TPU v7x, 256 devices: a whole 4x4x8 slice. The times are simulated.
256 devices in a mesh: ap: 32 (over z, y_hi, core), tm: 8 (over x, y_lo).
Axes of the slice: x: 4, y: 4 (y_hi: 2, y_lo: 2; y = y_hi * 2 + y_lo), z: 8, core: 2. Of those that a mesh axis runs over, the one named last changes fastest.
Arguments:
- voltages: bfloat16 [128, 64, 128, 256], P('tm', None, 'ap'), may hold values from -6 to 6
Outputs:
- visibility: float32 [256, 2, 64, 256], P('tm', None, 'ap')
All inputs are finite; a program needn't handle non-finite values.
Results may differ from a plain program's by a relative error of at most 0.012.
Values may be sent and summed in bfloat16 or wider, within the bound.
No kernel may reach another device: no remote copies, remote signals or barrier semaphores. Data moves between devices by JAX's collectives and lax.ppermute only.
A program may use at most 128 MiB of HBM per device.

v0:
```python
import math

import jax
import jax.numpy as jnp
from jax import lax
from jax.sharding import PartitionSpec as P

two_pi = 2.0 * math.pi


def column_table(grid_side, pad_side):
    dishes = jnp.arange(grid_side, dtype=jnp.int32)
    columns = jnp.arange(pad_side, dtype=jnp.int32)
    angle = (dishes[:, None] * columns[None, :] % pad_side).astype(jnp.float32) * (
        two_pi / pad_side
    )
    cosine = jnp.cos(angle)
    sine = jnp.sin(angle)
    upper = jnp.concatenate([cosine, -sine], axis=1)
    lower = jnp.concatenate([sine, cosine], axis=1)
    return jnp.concatenate([upper, lower], axis=0).astype(jnp.bfloat16)


def row_table(grid_side, pad_side):
    beams = jnp.arange(pad_side, dtype=jnp.int32)
    dishes = jnp.arange(grid_side, dtype=jnp.int32)
    angle = (beams[:, None] * dishes[None, :] % pad_side).astype(jnp.float32) * (two_pi / pad_side)
    return jnp.concatenate([jnp.cos(angle), jnp.sin(angle)], axis=0).astype(jnp.bfloat16)


def lag_table(pad_side):
    index = jnp.arange(pad_side, dtype=jnp.int32)
    angle = (index[:, None] * index[None, :] % pad_side).astype(jnp.float32) * (two_pi / pad_side)
    return jnp.concatenate([jnp.cos(angle), jnp.sin(angle)], axis=1)


def power_of(mixed, pad_side):
    beam_real = mixed[..., :pad_side, :pad_side] + mixed[..., pad_side:, pad_side:]
    beam_imag = mixed[..., :pad_side, pad_side:] - mixed[..., pad_side:, :pad_side]
    return beam_real * beam_real + beam_imag * beam_imag


def finish(raw, lag_rows, grid_side, pad_side, samples):
    lag_cols = jnp.arange(pad_side, dtype=jnp.int32)
    signed_rows = jnp.where(lag_rows < grid_side, lag_rows, lag_rows - pad_side)
    signed_cols = jnp.where(lag_cols < grid_side, lag_cols, lag_cols - pad_side)
    pairs_rows = jnp.maximum(grid_side - jnp.abs(signed_rows), 0)
    pairs_cols = jnp.maximum(grid_side - jnp.abs(signed_cols), 0)
    count = pairs_rows[:, None] * pairs_cols[None, :]
    keep = (count > 0) & jnp.logical_not((lag_rows[:, None] == 0) & (lag_cols[None, :] == 0))
    denom = float(pad_side * pad_side) * jnp.sqrt(
        jnp.maximum(count, 1).astype(jnp.float32) * float(samples)
    )
    factor = jnp.where(keep, 1.0 / denom, 0.0)
    return raw * factor[:, None, None, :]


def lag_terms(half, first_row, count, pad_side):
    lag_rows = jnp.arange(count, dtype=jnp.int32)
    beam_rows = first_row + jnp.arange(half.shape[1], dtype=jnp.int32)
    angle = (lag_rows[:, None] * beam_rows[None, :] % pad_side).astype(jnp.float32) * (
        two_pi / pad_side
    )
    first_sum = jnp.einsum("lu,cuj->lcj", jnp.cos(angle), half, precision=lax.Precision.HIGHEST)
    second_sum = jnp.einsum("lu,cuj->lcj", jnp.sin(angle), half, precision=lax.Precision.HIGHEST)
    vis_real = first_sum[..., :pad_side] - second_sum[..., pad_side:]
    vis_imag = first_sum[..., pad_side:] + second_sum[..., :pad_side]
    return jnp.stack([vis_real, vis_imag], axis=1)


def shards(voltages):
    samples, channels, local_rows, twice = voltages.shape
    grid_side = twice // 2
    pad_side = 2 * grid_side
    first = column_table(grid_side, pad_side)
    second = row_table(grid_side, pad_side)
    total_samples = samples * lax.axis_size("tm")
    lead = voltages.shape[:3]
    field = jnp.dot(voltages.reshape(-1, twice), first, preferred_element_type=jnp.float32)
    field = field.astype(jnp.bfloat16).reshape(lead + (2 * pad_side,))
    beam_field = lax.all_to_all(field, "ap", split_axis=1, concat_axis=2, tiled=True)
    mixed = jnp.einsum("wr,tcrk->tcwk", second, beam_field, preferred_element_type=jnp.float32)
    powers = power_of(mixed, pad_side)
    partial_value = jnp.sum(powers, axis=0)
    table = lag_table(pad_side)
    owned = pad_side // lax.axis_size("tm")
    share = lax.psum_scatter(partial_value, "tm", scatter_dimension=1, tiled=True)
    half = jnp.einsum("cuk,kj->cuj", share, table, precision=lax.Precision.HIGHEST)
    first_row = lax.axis_index("tm") * owned
    raw = lax.psum_scatter(
        lag_terms(half, first_row, owned * lax.axis_size("tm"), pad_side),
        "tm",
        scatter_dimension=0,
        tiled=True,
    )
    lag_rows = lax.axis_index("tm") * owned + jnp.arange(owned, dtype=jnp.int32)
    return finish(raw, lag_rows, grid_side, pad_side, total_samples)


def solution(mesh):
    in_specs = (P("tm", None, "ap", None),)
    out_specs = P("tm", None, "ap", None)
    return jax.shard_map(shards, mesh=mesh, in_specs=in_specs, out_specs=out_specs, check_vma=False)
```

profile of v0, /device:TPU:16, one launch (start us, length us, event | category | flops | bytes accessed | tf_op | source)
XLA Modules:
  0.0 304.6 jit_solution(12651816762852626518)
XLA Ops:
  6.5 0.5 negate_convert_fusion
  7.1 0.5 fusion.42
  7.6 2.6 reshape.96
  10.1 3.3 %fusion.4 = bf16[4096,512]{0,1:T(8,128)(2,1)} fusion(bf16[4096,256]{1,0:T(8,128)(2,1)S(1)} %reshape.96, bf16[128,256]{1,0:T(8,128)(2,1)S(1)} %get-tuple-element.8, bf16[128,256]{1,0:T(8,128)(2,1)S(1)} %fusion.42, bf16[128,256]{1,0:T(8,128)(2,1)S(1)} %get-tuple-element.7), kind=kOutput, calls=%fused_computation.8 | convolution fusion | flops 1076887552 | bytes 6488064 | tf_op jit(solution)/shard_map/dot_general | solution.py:79
  13.4 6.5 %copy.20 = bf16[4096,512]{1,0:T(8,128)(2,1)} copy(bf16[4096,512]{0,1:T(8,128)(2,1)} %fusion.4) | data formatting | bytes 8388608 | tf_op jit(solution)/shard_map/convert_element_type | solution.py:80
  19.9 7.0 %reshape.97 = bf16[16,64,4,512]{3,2,1,0:T(4,128)(2,1)} reshape(bf16[4096,512]{1,0:T(8,128)(2,1)} %copy.20) | data formatting | bytes 8388608 | tf_op jit(solution)/shard_map/reshape | solution.py:80
  26.8 6.4 %copy.21 = bf16[16,64,4,512]{3,2,0,1:T(4,128)(2,1)} copy(bf16[16,64,4,512]{3,2,1,0:T(4,128)(2,1)} %reshape.97) | data formatting | bytes 8388608 | tf_op jit(solution)/shard_map/reshape | solution.py:80
  33.3 11.6 %all-to-all-start = ((bf16[16,64,4,512]{3,2,0,1:T(4,128)(2,1)}), bf16[16,64,4,512]{3,2,0,1:T(4,128)(2,1)}, u32[]{:S(2)}, u32[]{:S(2)}) async-start(bf16[16,64,4,512]{3,2,0,1:T(4,128)(2,1)} %copy.21), calls=%async_computation | async-start | bytes 8388608 | tf_op jit(solution)/shard_map/all_to_all | solution.py:81
  44.9 0.2 all-reduce.3.cloned.1.call-start
  45.2 0.5 sine_convert_fusion
  45.7 93.3 %all-to-all-done = bf16[16,64,4,512]{3,2,0,1:T(4,128)(2,1)} async-done(((bf16[16,64,4,512]{3,2,0,1:T(4,128)(2,1)}), bf16[16,64,4,512]{3,2,0,1:T(4,128)(2,1)}, u32[]{:S(2)}, u32[]{:S(2)}) %all-to-all-start) | async-done | bytes 4194336 | tf_op jit(solution)/shard_map/all_to_all | solution.py:81
  139.0 3.6 %copy.22 = bf16[16,64,4,512]{3,0,2,1:T(8,128)(2,1)S(1)} copy(bf16[16,64,4,512]{3,2,0,1:T(4,128)(2,1)} %all-to-all-done) | data formatting | bytes 8388608 | tf_op jit(solution)/shard_map/all_to_all | solution.py:81
  142.6 0.5 copy.23
  143.1 14.6 %convolution_bitcast_fusion = f32[16,2,512,512]{2,3,1,0:T(8,128)} fusion(bf16[16,2,128,512]{3,0,2,1:T(8,128)(2,1)S(1)} %bitcast.30, bf16[256,128]{1,0:T(8,128)(2,1)S(1)} %get-tuple-element.9, bf16[256,128]{1,0:T(8,128)(2,1)S(1)} %get-tuple-element.10), kind=kOutput, calls=%fused_computation | convolution fusion | flops 2147745792 | bytes 37879808 | tf_op jit(solution)/shard_map/wr,tcrk->tcwk/dot_general | solution.py:82
  157.6 0.0 copy-start
  157.6 12.4 %fusion.2 = f32[2,256,256]{1,2,0:T(8,128)S(1)} fusion(f32[16,2,512,512]{2,3,1,0:T(8,128)} %convolution_bitcast_fusion), kind=kLoop, calls=%fused_computation.4 | loop fusion | flops 12451840 | bytes 34078720 | tf_op jit(solution)/shard_map/reduce_sum | solution.py:84
  170.1 1.0 copy.25
  171.1 0.0 all-reduce.3.cloned.1.call-update
  171.1 0.0 reduce-scatter.2.cloned.1.call-start
  171.2 0.0 copy-done
  171.2 0.6 dynamic-slice
  172.4 1.0 fusion.32
  173.5 76.0 %all-reduce.3.cloned.1.call-done = f32[2,256,256]{2,0,1:T(2,128)} async-done(((f32[2,256,256]{2,0,1:T(2,128)}), f32[2,256,256]{2,0,1:T(2,128)}) %all-reduce.3.cloned.1.call-update) | async-done | bytes 524304
  249.5 0.8 constant_dynamic-slice_fusion
  250.3 0.4 fusion.8
  250.7 1.2 fusion.52
  252.0 1.2 fusion.54
  253.2 0.1 fusion.7
  253.3 1.0 pad_maximum_fusion
  254.4 0.0 reduce-scatter.2.cloned.1.call-update
  254.4 0.1 fusion.48
  254.5 41.6 %reduce-scatter.2.cloned.1.call-done = f32[32,2,2,256]{3,0,2,1:T(8,128)} async-done(((f32[256,2,2,256]{3,0,2,1:T(8,128)}), f32[32,2,2,256]{3,0,2,1:T(8,128)}) %reduce-scatter.2.cloned.1.call-update) | async-done | bytes 131088 | tf_op jit(solution)/shard_map/reduce_scatter | solution.py:90
  296.1 0.9 broadcast_multiply_fusion
  297.0 0.8 copy.27
  (5 shorter events, 0.0 us)
Async XLA Ops:
  33.3 105.7 %all-to-all-start = ((bf16[16,64,4,512]{3,2,0,1:T(4,128)(2,1)}), bf16[16,64,4,512]{3,2,0,1:T(4,128)(2,1)}, u32[]{:S(2)}, u32[]{:S(2)}) async-start(bf16[16,64,4,512]{3,2,0,1:T(4,128)(2,1)} %copy.21), calls=%async_computation | async-start | bytes 8388608 | tf_op jit(solution)/shard_map/all_to_all | solution.py:81
  44.9 204.5 %all-reduce.3.cloned.1.call-start = ((), (), s32[]{:S(2)}) async-start(), calls=%async_computation.3 | async-start | bytes 1048576
  157.6 13.5 %copy-start = (u32[256]{0:T(256)S(1)}, u32[256]{0:T(256)}, u32[]{:S(2)}) copy-start(u32[256]{0:T(256)} %constant.76) | copy-start | bytes 3076
  171.1 125.0 %reduce-scatter.2.cloned.1.call-start = ((), (), s32[]{:S(2)}) async-start(), calls=%async_computation.2 | async-start | bytes 1179648 | tf_op jit(solution)/shard_map/reduce_scatter | solution.py:90
Sparse Core Ops, SparseCore 0:
  171.2 78.1 all-reduce.2
  254.5 41.5 reduce-scatter.1
where the time goes:
time: 305 us
  waiting for transfers between devices  211 us (69%)
  local copies, waits for them, and re-layouts  29.6 us (10%)
  matrix products  20.7 us (7%)
  other arithmetic  17.3 us (6%)
  between operations  14.2 us (5%)
  starting transfers between devices  11.9 us (4%)
    all_to_all x1, waiting for transfers between devices, shards(): lax.all_to_all(field, 'ap', split_axis=1, concat_axis=2, tiled=True)  93.3 us
    unnamed x3, waiting for transfers between devices  76 us
    reduce_scatter x1, waiting for transfers between devices, shards(): lax.psum_scatter(lag_terms(half, first_row, owned * lax.axis_size('tm'),...  41.6 us
    dot_general x1, matrix products, shards(): jnp.einsum('wr,tcrk->tcwk', second, beam_field, preferred_element_type=jn...  14.6 us
    reshape x2, local copies, waits for them, and re-layouts, shards(): field = field.astype(jnp.bfloat16).reshape(lead + (2 * pad_side,))  13.4 us
    reduce_sum x1, other arithmetic, shards(): partial_value = jnp.sum(powers, axis=0)  12.4 us
    all_to_all x1, starting transfers between devices, shards(): lax.all_to_all(field, 'ap', split_axis=1, concat_axis=2, tiled=True)  11.6 us
    convert_element_type x1, local copies, waits for them, and re-layouts, shards(): field = field.astype(jnp.bfloat16).reshape(lead + (2 * pad_side,))  6.47 us
  transfers between devices with their start and end apart: 3, of which 3 were waited for; matrix products, arithmetic and copies ran while one was open for 1% of the time, Pallas kernels for 0%

commit v1 on v0

v1 whole, which is shorter than its diff:
```python
import functools
import math

import jax
import jax.numpy as jnp
import numpy as np
from jax import lax
from jax.experimental import pallas as pl
from jax.experimental.pallas import tpu as pltpu
from jax.sharding import PartitionSpec as P

F32 = jnp.float32
BF16 = jnp.bfloat16


def angles(rows, cols, pad_side):
    return (rows[:, None] * cols[None, :] % pad_side) * (2.0 * math.pi / pad_side)


def split(table):
    high = table.astype(BF16)
    low = (table - high.astype(np.float32)).astype(BF16)
    return high, low


def tables(grid_side, pad_side, samples):
    dishes, index = np.arange(grid_side), np.arange(pad_side)
    columns = angles(dishes, index, pad_side)
    cosine, sine = np.cos(columns), np.sin(columns)
    first = np.concatenate(
        [np.concatenate([cosine, -sine], 1), np.concatenate([sine, cosine], 1)], 0
    ).astype(BF16)
    second = np.concatenate([cosine.T, sine.T], 1).astype(BF16)
    whole = angles(index, index, pad_side)
    lag = np.concatenate([np.cos(whole), np.sin(whole)], 1).astype(np.float32)
    signed = np.where(index < grid_side, index, index - pad_side)
    pairs = np.maximum(grid_side - np.abs(signed), 0)
    count = pairs[:, None] * pairs[None, :]
    keep = (count > 0) & ((index[:, None] > 0) | (index[None, :] > 0))
    scale = 1.0 / (float(pad_side * pad_side) * np.sqrt(np.maximum(count, 1) * float(samples)))
    factor = np.where(keep, scale, 0.0).astype(np.float32)
    return first, second, *split(lag), factor


def dot(a, b):
    return jnp.dot(a, b, preferred_element_type=F32)


def halves(value):
    high = value.astype(BF16)
    return high, (value - high.astype(F32)).astype(BF16)


def dot3(a, b):
    return dot(a[0], b[0]) + (dot(a[0], b[1]) + dot(a[1], b[0]))


def correlate(v_ref, first_ref, second_ref, lag_hi_ref, lag_lo_ref, factor_ref, out_ref, power_ref):
    samples, channels = v_ref.shape[:2]
    pad = second_ref.shape[0]
    owned = out_ref.shape[3]
    power_ref[...] = jnp.zeros_like(power_ref)

    def sample(t, carry):
        for c in range(channels):
            field = dot(v_ref[t, c], first_ref[...]).astype(BF16)
            real, imag = field[:, :pad], field[:, pad:]
            stacked = jnp.concatenate(
                [jnp.concatenate([real, imag], 1), jnp.concatenate([imag, -real], 1)], 0
            )
            beam = dot(second_ref[...], stacked)
            power_ref[c] += beam[:, :pad] * beam[:, :pad] + beam[:, pad:] * beam[:, pad:]
        return carry

    lax.fori_loop(0, samples, sample, 0)
    lag = (lag_hi_ref[...], lag_lo_ref[...])
    for c in range(channels):
        half = dot3(halves(power_ref[c]), lag)
        real, imag = half[:, :pad], half[:, pad:]
        stacked = jnp.concatenate(
            [jnp.concatenate([real, imag], 1), jnp.concatenate([-imag, real], 1)], 0
        )
        raw = dot3(lag, halves(stacked))
        for part in range(2):
            terms = (raw[:, part * pad : (part + 1) * pad] * factor_ref[...]).astype(BF16)
            out_ref[:, part, c] = terms.reshape(pad // owned, owned, pad)


def shards(voltages):
    samples, channels, local_rows, twice = voltages.shape
    grid_side = twice // 2
    pad_side = 2 * grid_side
    over_ap, over_tm = lax.axis_size("ap"), lax.axis_size("tm")
    own = channels // over_ap
    owned = pad_side // over_tm
    consts = tables(grid_side, pad_side, samples * over_tm)
    sent = voltages.reshape(samples, over_ap, own, local_rows, twice).transpose(1, 0, 2, 3, 4)
    got = lax.all_to_all(sent, "ap", 0, 0, tiled=True)
    rows = got.transpose(1, 2, 0, 3, 4).reshape(samples, own, grid_side, twice)
    terms = pl.pallas_call(
        correlate,
        out_shape=jax.ShapeDtypeStruct((over_tm, 2, own, owned, pad_side), BF16),
        in_specs=[pl.BlockSpec(memory_space=pltpu.VMEM)] * 6,
        out_specs=pl.BlockSpec(memory_space=pltpu.VMEM),
        scratch_shapes=[pltpu.VMEM((own, pad_side, pad_side), F32)],
        compiler_params=pltpu.CompilerParams(vmem_limit_bytes=40 * 1024 * 1024),
        name="correlate",
    )(rows, *[jnp.asarray(c) for c in consts])
    parts = lax.all_to_all(terms, "tm", 0, 0, tiled=True)
    return jnp.sum(parts.astype(F32), axis=0).transpose(2, 0, 1, 3)


def solution(mesh):
    in_specs = (P("tm", None, "ap", None),)
    out_specs = P("tm", None, "ap", None)
    return jax.shard_map(shards, mesh=mesh, in_specs=in_specs, out_specs=out_specs, check_vma=False)
```

time: 305 us -> 100 us (0.33)
  waiting for transfers between devices: 211 us -> 0 us
  blocking collectives: 0 us -> 77 us
  matrix products: 20.7 us -> 0 us
  local copies, waits for them, and re-layouts: 29.6 us -> 10.8 us
  other arithmetic: 17.3 us -> 0.08 us
  between operations: 14.2 us -> 0.08 us
  Pallas kernels: 0 us -> 12.2 us
  starting transfers between devices: 11.9 us -> 0 us
    all_to_all x1 -> x0, waiting for transfers between devices: 93.3 us -> none  [shards(): lax.all_to_all(field, 'ap', split_axis=1, concat_axis=2, tiled=True)]
    all_to_all x0 -> x2, blocking collectives: none -> 77 us  [the longest x1 62.8 us: shards(): got = lax.all_to_all(sent, 'ap', 0, 0, tiled=True)]
    unnamed x3 -> x0, waiting for transfers between devices: 76 us -> none
    reduce_scatter x1 -> x0, waiting for transfers between devices: 41.6 us -> none  [shards(): lax.psum_scatter(lag_terms(half, first_row, owned * lax.axis_size('tm'),...]
    dot_general x5 -> x0, matrix products: 20.7 us -> none  [the longest x1 14.6 us: shards(): jnp.einsum('wr,tcrk->tcwk', second, beam_field, preferred_element_type=jn...]
    reshape x3 -> x1, local copies, waits for them, and re-layouts: 15.9 us -> 2.64 us  [shards(): rows = got.transpose(1, 2, 0, 3, 4).reshape(samples, own, grid_side, twice)]
    reduce_sum x1, other arithmetic: 12.4 us -> 0.08 us  [shards(): return jnp.sum(parts.astype(F32), axis=0).transpose(2, 0, 1, 3)]
    pallas_call x0 -> x1, Pallas kernels: none -> 12.2 us  [shards(): pl.pallas_call(correlate, out_shape=jax.ShapeDtypeStruct((over_tm, 2, own...]
  transfers between devices with their start and end apart: 3 -> 0, of which waited for: 3 -> 0; matrix products, arithmetic and copies ran while one was open for 1% -> 0% of each run, Pallas kernels for 0% -> 0%
where the time goes in v1:
time: 100 us
  blocking collectives  77 us (77%)
  Pallas kernels  12.2 us (12%)
  local copies, waits for them, and re-layouts  10.8 us (11%)
    all_to_all x1, blocking collectives, shards(): got = lax.all_to_all(sent, 'ap', 0, 0, tiled=True)  62.8 us
    all_to_all x1, blocking collectives, shards(): parts = lax.all_to_all(terms, 'tm', 0, 0, tiled=True)  14.2 us
    pallas_call x1, Pallas kernels, shards(): pl.pallas_call(correlate, out_shape=jax.ShapeDtypeStruct((over_tm, 2, own...  12.2 us
    unnamed x11, local copies, waits for them, and re-layouts  3.86 us
    reshape x1, local copies, waits for them, and re-layouts, shards(): rows = got.transpose(1, 2, 0, 3, 4).reshape(samples, own, grid_side, twice)  2.64 us
    transpose x1, local copies, waits for them, and re-layouts, shards(): rows = got.transpose(1, 2, 0, 3, 4).reshape(samples, own, grid_side, twice)  2.45 us

profile of v1, /device:TPU:16, one launch (start us, length us, event | category | flops | bytes accessed | tf_op | source)
XLA Modules:
  0.0 100.1 jit_solution(584462286277493895)
XLA Ops:
  0.0 3.8 %copy.10 = bf16[16,64,4,256]{3,0,2,1:T(8,128)(2,1)S(1)} copy(bf16[16,64,4,256]{3,2,1,0:T(4,128)(2,1)} %param.6) | data formatting | bytes 4194304 | tf_op args[0]
  3.8 1.1 %copy.11 = bf16[32,16,2,4,256]{4,3,2,1,0:T(4,128)(2,1)S(1)} copy(bf16[32,16,2,4,256]{4,1,3,2,0:T(8,128)(2,1)S(1)} %bitcast.6) | data formatting | bytes 4194304 | tf_op jit(solution)/shard_map/transpose | solution.py:97
  4.9 62.8 %all_to_all.10 = bf16[32,16,2,4,256]{4,3,2,1,0:T(4,128)(2,1)S(1)} all-to-all(bf16[32,16,2,4,256]{4,3,2,1,0:T(4,128)(2,1)S(1)} %copy.11), channel_id=1, replica_groups=mesh['ap'=32,'tm'=8] {'ap'}, dimensions={0} | all-to-all | bytes 4194304 | tf_op jit(solution)/shard_map/all_to_all | solution.py:98
  67.7 2.5 %copy.12 = bf16[16,2,32,4,256]{4,3,2,1,0:T(4,128)(2,1)} copy(bf16[16,2,32,4,256]{4,3,1,0,2:T(4,128)(2,1)S(1)} %bitcast.5) | data formatting | bytes 4194304 | tf_op jit(solution)/shard_map/transpose | solution.py:99
  70.2 0.0 copy-start
  70.2 0.0 copy-start.1
  70.2 0.0 copy-start.2
  70.2 0.0 copy-start.3
  70.2 0.0 copy-start.4
  70.2 2.6 %reshape.7.v_ref = bf16[16,2,128,256]{3,2,1,0:T(8,128)(2,1)S(1)} reshape(bf16[16,2,32,4,256]{4,3,2,1,0:T(4,128)(2,1)} %copy.12) | data formatting | bytes 4194304 | tf_op jit(solution)/shard_map/reshape | solution.py:99
  72.9 0.0 copy-done
  72.9 0.0 copy-done.1
  72.9 0.0 copy-done.2
  72.9 0.0 copy-done.3
  72.9 0.0 copy-done.4
  72.9 12.2 %correlate.1 = bf16[8,2,2,32,256]{4,3,2,1,0:T(8,128)(2,1)S(1)} custom-call(bf16[16,2,128,256]{3,2,1,0:T(8,128)(2,1)S(1)} %reshape.7.v_ref, bf16[256,512]{1,0:T(8,128)(2,1)S(1)} %copy-done.3, bf16[256,256]{1,0:T(8,128)(2,1)S(1)} %copy-done.4, bf16[256,512]{1,0:T(8,128)(2,1)S(1)} %copy-done.2, bf16[256,512]{1,0:T(8,128)(2,1)S(1)} %copy-done.1, ...), custom_call_target="tpu_custom_call" | custom-call | tf_op jit(solution)/shard_map/correlate/pallas_call | solution.py:100
  85.1 14.2 %all_to_all.11 = bf16[8,2,2,32,256]{4,3,2,1,0:T(8,128)(2,1)S(1)} all-to-all(bf16[8,2,2,32,256]{4,3,2,1,0:T(8,128)(2,1)S(1)} %correlate.1), channel_id=1, replica_groups=mesh['ap'=32,'tm'=8] {'tm'}, dimensions={0} | all-to-all | bytes 1048576 | tf_op jit(solution)/shard_map/all_to_all | solution.py:109
  99.3 0.1 convert_reduce_fusion
  99.4 0.8 copy.13
Async XLA Ops:
  70.2 2.7 %copy-start = (f32[256,256]{1,0:T(8,128)S(1)}, f32[256,256]{1,0:T(8,128)}, u32[]{:S(2)}) copy-start(f32[256,256]{1,0:T(8,128)} %constant.16.clone.factor_ref) | copy-start | bytes 786436
  70.2 2.7 %copy-start.1 = (bf16[256,512]{1,0:T(8,128)(2,1)S(1)}, bf16[256,512]{1,0:T(8,128)(2,1)}, u32[]{:S(2)}) copy-start(bf16[256,512]{1,0:T(8,128)(2,1)} %constant.15.clone.lag_lo_ref) | copy-start | bytes 786436
  70.2 2.7 %copy-start.2 = (bf16[256,512]{1,0:T(8,128)(2,1)S(1)}, bf16[256,512]{1,0:T(8,128)(2,1)}, u32[]{:S(2)}) copy-start(bf16[256,512]{1,0:T(8,128)(2,1)} %constant.14.clone.lag_hi_ref) | copy-start | bytes 786436
  70.2 2.7 %copy-start.3 = (bf16[256,512]{1,0:T(8,128)(2,1)S(1)}, bf16[256,512]{1,0:T(8,128)(2,1)}, u32[]{:S(2)}) copy-start(bf16[256,512]{1,0:T(8,128)(2,1)} %constant.12.clone.first_ref) | copy-start | bytes 786436
  70.2 2.7 %copy-start.4 = (bf16[256,256]{1,0:T(8,128)(2,1)S(1)}, bf16[256,256]{1,0:T(8,128)(2,1)}, u32[]{:S(2)}) copy-start(bf16[256,256]{1,0:T(8,128)(2,1)} %constant.13.clone.second_ref) | copy-start | bytes 393220

commit v2 on v1

v2 whole, which is shorter than its diff:
```python
import functools
import math

import jax
import jax.numpy as jnp
import numpy as np
from jax import lax
from jax.experimental import pallas as pl
from jax.experimental.pallas import tpu as pltpu
from jax.sharding import PartitionSpec as P

F32 = jnp.float32
BF16 = jnp.bfloat16
VMEM_BYTES = 48 * 1024 * 1024


def angles(rows, cols, pad_side):
    return (rows[:, None] * cols[None, :] % pad_side) * (2.0 * math.pi / pad_side)


def split(table):
    table = table.astype(np.float32)
    high = table.astype(BF16)
    return high, (table - high.astype(np.float32)).astype(BF16)


def tables(grid_side, pad_side, samples):
    dishes, index = np.arange(grid_side), np.arange(pad_side)
    padded = angles(dishes, index, pad_side)
    cosine, sine = np.cos(padded), np.sin(padded)
    first = np.block([[cosine, -sine], [sine, cosine]]).astype(BF16)
    second = np.block([[cosine.T, sine.T], [-sine.T, cosine.T]]).astype(BF16)
    by_row = split(np.concatenate([cosine, sine], 0))
    whole = angles(index, index, pad_side)
    by_col = split(np.concatenate([np.cos(whole), np.sin(whole)], 1))
    signed = np.where(index < grid_side, index, index - pad_side)
    pairs = np.maximum(grid_side - np.abs(signed), 0)
    count = pairs[:, None] * pairs[None, :]
    keep = (count > 0) & ((index[:, None] > 0) | (index[None, :] > 0))
    scale = 1.0 / (float(pad_side * pad_side) * np.sqrt(np.maximum(count, 1) * float(samples)))
    factor = np.where(keep, scale, 0.0).astype(np.float32)[:grid_side]
    flip = (dishes[:, None] + dishes[None, :] == grid_side).astype(BF16)
    return first, second, *by_row, *by_col, factor, flip


def dot(a, b):
    return jnp.dot(a, b, preferred_element_type=F32)


def halves(value):
    high = value.astype(BF16)
    return high, (value - high.astype(F32)).astype(BF16)


def dot3(a, b):
    return dot(a[0], b[0]) + (dot(a[0], b[1]) + dot(a[1], b[0]))


def pack(x_ref, out_ref, sems):
    copies = [
        pltpu.make_async_copy(x_ref.at[:, d], out_ref.at[d], sems.at[d])
        for d in range(out_ref.shape[0])
    ]
    for copy in copies:
        copy.start()
    for copy in copies:
        copy.wait()


def rows_of(got_ref, t, c):
    blocks = got_ref[:, t, c].astype(F32)
    count, both, lanes = blocks.shape
    pairs = blocks.reshape(count // 2, 2, both, lanes)
    even, odd = pairs[:, 0], pairs[:, 1]
    upper = lax.broadcasted_iota(jnp.int32, even.shape, 1) < both // 2
    real = jnp.where(upper, even, pltpu.roll(odd, both // 2, 1))
    imag = jnp.where(upper, pltpu.roll(even, both // 2, 1), odd)
    rows = count * both // 2
    return jnp.concatenate([real.reshape(rows, lanes), imag.reshape(rows, lanes)], 1).astype(BF16)


def correlate(
    batch, got_ref, first_ref, second_ref, row_hi, row_lo, col_hi, col_lo, factor_ref, flip_ref, out_ref, power_ref
):
    samples, channels = got_ref.shape[1:3]
    pad = second_ref.shape[1]
    grid_side = pad // 2
    owned = out_ref.shape[3]
    near = grid_side // owned
    power_ref[...] = jnp.zeros_like(power_ref)

    def step(i, carry):
        rows = [rows_of(got_ref, i * batch + t, c) for c in range(channels) for t in range(batch)]
        field = dot(jnp.concatenate(rows, 0), first_ref[...]).astype(BF16)
        for c in range(channels):
            total = power_ref[c]
            for t in range(batch):
                one = field[(c * batch + t) * grid_side : (c * batch + t + 1) * grid_side]
                beam = dot(second_ref[...], jnp.concatenate([one[:, :pad], one[:, pad:]], 0))
                total += beam[:pad] * beam[:pad] + beam[pad:] * beam[pad:]
            power_ref[c] = total
        return carry

    lax.fori_loop(0, samples // batch, step, 0)
    for c in range(channels):
        half = dot3((row_hi[...], row_lo[...]), halves(power_ref[c]))
        both = dot3(halves(half), (col_hi[...], col_lo[...]))
        cos_cos, cos_sin = both[:grid_side, :pad], both[:grid_side, pad:]
        sin_cos, sin_sin = both[grid_side:, :pad], both[grid_side:, pad:]
        plus = (cos_cos - sin_sin, cos_sin + sin_cos)
        minus = (cos_cos + sin_sin, cos_sin - sin_cos)
        for part in range(2):
            lower = (plus[part] * factor_ref[...]).astype(BF16)
            upper = dot(flip_ref[...], (minus[part] * factor_ref[...]).astype(BF16)).astype(BF16)
            out_ref[:near, part, c] = lower.reshape(near, owned, pad)
            out_ref[near:, part, c] = upper.reshape(near, owned, pad)


def shards(voltages):
    samples, channels, local_rows, twice = voltages.shape
    grid_side = twice // 2
    pad_side = 2 * grid_side
    over_ap, over_tm = lax.axis_size("ap"), lax.axis_size("tm")
    own = channels // over_ap
    owned = pad_side // over_tm
    consts = tables(grid_side, pad_side, samples * over_tm)
    vmem = pl.BlockSpec(memory_space=pltpu.VMEM)
    params = pltpu.CompilerParams(vmem_limit_bytes=VMEM_BYTES)
    view = voltages.reshape(samples, over_ap, own, local_rows, 2, grid_side)
    view = view.transpose(0, 1, 2, 4, 3, 5).reshape(samples, over_ap, own, 2 * local_rows, grid_side)
    sent = pl.pallas_call(
        pack,
        out_shape=jax.ShapeDtypeStruct((over_ap, samples) + view.shape[2:], BF16),
        in_specs=[pl.BlockSpec(memory_space=pl.ANY)],
        out_specs=vmem,
        scratch_shapes=[pltpu.SemaphoreType.DMA((over_ap,))],
        compiler_params=params,
        name="pack",
    )(view)
    got = lax.all_to_all(sent, "ap", 0, 0, tiled=True)
    terms = pl.pallas_call(
        functools.partial(correlate, math.gcd(samples, 8)),
        out_shape=jax.ShapeDtypeStruct((over_tm, 2, own, owned, pad_side), BF16),
        in_specs=[vmem] * (1 + len(consts)),
        out_specs=vmem,
        scratch_shapes=[pltpu.VMEM((own, pad_side, pad_side), F32)],
        compiler_params=params,
        name="correlate",
    )(got, *[jnp.asarray(c) for c in consts])
    parts = lax.all_to_all(terms, "tm", 0, 0, tiled=True)
    return jnp.sum(parts.astype(F32), axis=0).transpose(2, 0, 1, 3)


def solution(mesh):
    in_specs = (P("tm", None, "ap", None),)
    out_specs = P("tm", None, "ap", None)
    return jax.shard_map(shards, mesh=mesh, in_specs=in_specs, out_specs=out_specs, check_vma=False)
```

time: 100 us -> 85.9 us (0.86)
  local copies, waits for them, and re-layouts: 10.8 us -> 2.4 us
  Pallas kernels: 12.2 us -> 6.03 us
    pallas_call x1 -> x2, Pallas kernels: 12.2 us -> 6.03 us  [the longest x1 5.38 us: shards(): pl.pallas_call(functools.partial(correlate, math.gcd(samples, 8)), out_sh...]
    transpose x2 -> x0, local copies, waits for them, and re-layouts: 3.53 us -> none  [the longest x1 2.45 us: shards(): rows = got.transpose(1, 2, 0, 3, 4).reshape(samples, own, grid_side, twice)]
    reshape x1 -> x0, local copies, waits for them, and re-layouts: 2.64 us -> none  [shards(): rows = got.transpose(1, 2, 0, 3, 4).reshape(samples, own, grid_side, twice)]
    unnamed x11 -> x18, local copies, waits for them, and re-layouts: 3.86 us -> 1.65 us
where the time goes in v2:
time: 85.9 us; the launch traced here: 85.7 us
  blocking collectives  77.1 us (90%)
  Pallas kernels  6.03 us (7%)
  local copies, waits for them, and re-layouts  2.4 us (3%)
    all_to_all x1, blocking collectives, shards(): got = lax.all_to_all(sent, 'ap', 0, 0, tiled=True)  62.9 us
    all_to_all x1, blocking collectives, shards(): parts = lax.all_to_all(terms, 'tm', 0, 0, tiled=True)  14.2 us
    pallas_call x1, Pallas kernels, shards(): pl.pallas_call(functools.partial(correlate, math.gcd(samples, 8)), out_sh...  5.38 us

profile of v2, /device:TPU:16, one launch (start us, length us, event | category | flops | bytes accessed | tf_op | source)
XLA Modules:
  0.0 85.7 jit_solution(2050018535351309736)
XLA Ops:
  0.0 0.0 copy-start
  0.0 1.6 %copy-done = bf16[16,64,4,256]{3,2,1,0:T(4,128)(2,1)S(1)} copy-done((bf16[16,64,4,256]{3,2,1,0:T(4,128)(2,1)S(1)}, bf16[16,64,4,256]{3,2,1,0:T(4,128)(2,1)}, u32[]{:S(2)}) %copy-start) | copy-done | bytes 2097176
  1.6 0.7 pack.1
  2.3 0.0 copy-start.1
  2.3 0.0 copy-start.2
  2.3 0.0 copy-start.3
  2.3 0.0 copy-start.4
  2.3 0.0 copy-start.5
  2.3 0.0 copy-start.6
  2.3 0.0 copy-start.7
  2.3 0.0 copy-start.8
  2.4 62.9 %all_to_all.10.got_ref = bf16[32,16,2,8,128]{4,3,2,1,0:T(8,128)(2,1)S(1)} all-to-all(bf16[32,16,2,8,128]{4,3,2,1,0:T(8,128)(2,1)S(1)} %pack.1), channel_id=1, replica_groups=mesh['ap'=32,'tm'=8] {'ap'}, dimensions={0} | all-to-all | bytes 4194304 | tf_op jit(solution)/shard_map/all_to_all | solution.py:140
  65.3 0.0 copy-done.1
  65.3 0.0 copy-done.2
  65.3 0.0 copy-done.3
  65.3 0.0 copy-done.4
  65.3 0.0 copy-done.5
  65.3 0.0 copy-done.6
  65.3 0.0 copy-done.7
  65.3 0.0 copy-done.8
  65.3 5.4 %correlate.1 = bf16[8,2,2,32,256]{4,3,2,1,0:T(8,128)(2,1)S(1)} custom-call(bf16[32,16,2,8,128]{4,3,2,1,0:T(8,128)(2,1)S(1)} %all_to_all.10.got_ref, bf16[256,512]{1,0:T(8,128)(2,1)S(1)} %copy-done.4, bf16[512,256]{1,0:T(8,128)(2,1)S(1)} %copy-done.3, bf16[256,256]{1,0:T(8,128)(2,1)S(1)} %copy-done.7, bf16[256,256]{1,0:T(8,128)(2,1)S(1)} %copy-done.6, ...), custom_call_target="tpu_custom_call" | custom-call | tf_op jit(solution)/shard_map/correlate/pallas_call | solution.py:141
  70.7 14.2 %all_to_all.11 = bf16[8,2,2,32,256]{4,3,2,1,0:T(8,128)(2,1)S(1)} all-to-all(bf16[8,2,2,32,256]{4,3,2,1,0:T(8,128)(2,1)S(1)} %correlate.1), channel_id=1, replica_groups=mesh['ap'=32,'tm'=8] {'tm'}, dimensions={0} | all-to-all | bytes 1048576 | tf_op jit(solution)/shard_map/all_to_all | solution.py:150
  84.9 0.1 convert_reduce_fusion
  85.0 0.8 copy.12
Async XLA Ops:
  0.0 1.6 %copy-start = (bf16[16,64,4,256]{3,2,1,0:T(4,128)(2,1)S(1)}, bf16[16,64,4,256]{3,2,1,0:T(4,128)(2,1)}, u32[]{:S(2)}) copy-start(bf16[16,64,4,256]{3,2,1,0:T(4,128)(2,1)} %param.9) | copy-start | bytes 6291460
  2.3 63.0 %copy-start.1 = (bf16[256,512]{1,0:T(8,128)(2,1)S(1)}, bf16[256,512]{1,0:T(8,128)(2,1)}, u32[]{:S(2)}) copy-start(bf16[256,512]{1,0:T(8,128)(2,1)} %constant.23.clone.col_lo) | copy-start | bytes 786436
  2.3 63.0 %copy-start.2 = (bf16[256,512]{1,0:T(8,128)(2,1)S(1)}, bf16[256,512]{1,0:T(8,128)(2,1)}, u32[]{:S(2)}) copy-start(bf16[256,512]{1,0:T(8,128)(2,1)} %constant.22.clone.col_hi) | copy-start | bytes 786436
  2.3 63.0 %copy-start.3 = (bf16[512,256]{1,0:T(8,128)(2,1)S(1)}, bf16[512,256]{1,0:T(8,128)(2,1)}, u32[]{:S(2)}) copy-start(bf16[512,256]{1,0:T(8,128)(2,1)} %constant.19.clone.second_ref) | copy-start | bytes 786436
  2.3 63.0 %copy-start.4 = (bf16[256,512]{1,0:T(8,128)(2,1)S(1)}, bf16[256,512]{1,0:T(8,128)(2,1)}, u32[]{:S(2)}) copy-start(bf16[256,512]{1,0:T(8,128)(2,1)} %constant.18.clone.first_ref) | copy-start | bytes 786436
  2.3 63.0 %copy-start.5 = (f32[128,256]{1,0:T(8,128)S(1)}, f32[128,256]{1,0:T(8,128)}, u32[]{:S(2)}) copy-start(f32[128,256]{1,0:T(8,128)} %constant.24.clone.factor_ref) | copy-start | bytes 393220
  2.3 63.0 %copy-start.6 = (bf16[256,256]{1,0:T(8,128)(2,1)S(1)}, bf16[256,256]{1,0:T(8,128)(2,1)}, u32[]{:S(2)}) copy-start(bf16[256,256]{1,0:T(8,128)(2,1)} %constant.21.clone.row_lo) | copy-start | bytes 393220
  2.3 63.0 %copy-start.7 = (bf16[256,256]{1,0:T(8,128)(2,1)S(1)}, bf16[256,256]{1,0:T(8,128)(2,1)}, u32[]{:S(2)}) copy-start(bf16[256,256]{1,0:T(8,128)(2,1)} %constant.20.clone.row_hi) | copy-start | bytes 393220
  2.3 63.0 %copy-start.8 = (bf16[128,128]{1,0:T(8,128)(2,1)S(1)}, bf16[128,128]{1,0:T(8,128)(2,1)}, u32[]{:S(2)}) copy-start(bf16[128,128]{1,0:T(8,128)(2,1)} %constant.25.clone.flip_ref) | copy-start | bytes 98308

commit v3 on v2

--- a/solution.py
+++ b/solution.py
@@ -1,4 +1,3 @@
-import functools
 import math
 
 import jax
@@ -79,41 +78,51 @@
     return jnp.concatenate([real.reshape(rows, lanes), imag.reshape(rows, lanes)], 1).astype(BF16)
 
 
+def power_of(got_ref, first_ref, second_ref, c):
+    samples = got_ref.shape[1]
+    pad = second_ref.shape[1]
+    grid_side = pad // 2
+    rows = [rows_of(got_ref, t, c) for t in range(samples)]
+    field = dot(jnp.concatenate(rows, 0), first_ref[...]).astype(BF16)
+    total = None
+    for t in range(samples):
+        one = field[t * grid_side : (t + 1) * grid_side]
+        beam = dot(second_ref[...], jnp.concatenate([one[:, :pad], one[:, pad:]], 0))
+        power = beam[:pad] * beam[:pad] + beam[pad:] * beam[pad:]
+        total = power if total is None else total + power
+    return total
+
+
 def correlate(
-    batch, got_ref, first_ref, second_ref, row_hi, row_lo, col_hi, col_lo, factor_ref, flip_ref, out_ref, power_ref
+    got_ref, first_ref, second_ref, row_hi, row_lo, col_hi, col_lo, factor_ref, flip_ref, out_ref, power_ref
 ):
-    samples, channels = got_ref.shape[1:3]
+    channels = got_ref.shape[2]
     pad = second_ref.shape[1]
     grid_side = pad // 2
     owned = out_ref.shape[3]
     near = grid_side // owned
-    power_ref[...] = jnp.zeros_like(power_ref)
-
-    def step(i, carry):
-        rows = [rows_of(got_ref, i * batch + t, c) for c in range(channels) for t in range(batch)]
-        field = dot(jnp.concatenate(rows, 0), first_ref[...]).astype(BF16)
-        for c in range(channels):
-            total = power_ref[c]
-            for t in range(batch):
-                one = field[(c * batch + t) * grid_side : (c * batch + t + 1) * grid_side]
-                beam = dot(second_ref[...], jnp.concatenate([one[:, :pad], one[:, pad:]], 0))
-                total += beam[:pad] * beam[:pad] + beam[pad:] * beam[pad:]
-            power_ref[c] = total
-        return carry
-
-    lax.fori_loop(0, samples // batch, step, 0)
     for c in range(channels):
-        half = dot3((row_hi[...], row_lo[...]), halves(power_ref[c]))
-        both = dot3(halves(half), (col_hi[...], col_lo[...]))
-        cos_cos, cos_sin = both[:grid_side, :pad], both[:grid_side, pad:]
-        sin_cos, sin_sin = both[grid_side:, :pad], both[grid_side:, pad:]
+        power_ref[c] = power_of(got_ref, first_ref, second_ref, c)
+    powers = jnp.concatenate([power_ref[c] for c in range(channels)], 1)
+    half = dot3((row_hi[...], row_lo[...]), halves(powers))
+    half = jnp.concatenate([half[:, c * pad : (c + 1) * pad] for c in range(channels)], 0)
+    both = dot3(halves(half), (col_hi[...], col_lo[...]))
+    mirrored = []
+    for c in range(channels):
+        one = both[c * pad : (c + 1) * pad]
+        cos_cos, cos_sin = one[:grid_side, :pad], one[:grid_side, pad:]
+        sin_cos, sin_sin = one[grid_side:, :pad], one[grid_side:, pad:]
         plus = (cos_cos - sin_sin, cos_sin + sin_cos)
         minus = (cos_cos + sin_sin, cos_sin - sin_cos)
         for part in range(2):
             lower = (plus[part] * factor_ref[...]).astype(BF16)
-            upper = dot(flip_ref[...], (minus[part] * factor_ref[...]).astype(BF16)).astype(BF16)
             out_ref[:near, part, c] = lower.reshape(near, owned, pad)
-            out_ref[near:, part, c] = upper.reshape(near, owned, pad)
+            mirrored.append((minus[part] * factor_ref[...]).astype(BF16))
+    upper = dot(flip_ref[...], jnp.concatenate(mirrored, 1)).astype(BF16)
+    for c in range(channels):
+        for part in range(2):
+            at = (2 * c + part) * pad
+            out_ref[near:, part, c] = upper[:, at : at + pad].reshape(near, owned, pad)
 
 
 def shards(voltages):
@@ -131,7 +140,7 @@
     sent = pl.pallas_call(
         pack,
         out_shape=jax.ShapeDtypeStruct((over_ap, samples) + view.shape[2:], BF16),
-        in_specs=[pl.BlockSpec(memory_space=pl.ANY)],
+        in_specs=[pl.BlockSpec(memory_space=pltpu.HBM)],
         out_specs=vmem,
         scratch_shapes=[pltpu.SemaphoreType.DMA((over_ap,))],
         compiler_params=params,
@@ -139,7 +148,7 @@
     )(view)
     got = lax.all_to_all(sent, "ap", 0, 0, tiled=True)
     terms = pl.pallas_call(
-        functools.partial(correlate, math.gcd(samples, 8)),
+        correlate,
         out_shape=jax.ShapeDtypeStruct((over_tm, 2, own, owned, pad_side), BF16),
         in_specs=[vmem] * (1 + len(consts)),
         out_specs=vmem,

time: 85.9 us -> 85 us (0.990)
  Pallas kernels: 6.03 us -> 5.07 us
    pallas_call x1, Pallas kernels: 5.38 us -> 4.42 us  [shards(): pl.pallas_call(correlate, out_shape=jax.ShapeDtypeStruct((over_tm, 2, own...]
where the time goes in v3:
time: 85 us; the launch traced here: 84.8 us
  blocking collectives  77.1 us (91%)
  Pallas kernels  5.07 us (6%)
  local copies, waits for them, and re-layouts  2.4 us (3%)
    all_to_all x1, blocking collectives, shards(): got = lax.all_to_all(sent, 'ap', 0, 0, tiled=True)  62.9 us
    all_to_all x1, blocking collectives, shards(): parts = lax.all_to_all(terms, 'tm', 0, 0, tiled=True)  14.2 us
    pallas_call x1, Pallas kernels, shards(): pl.pallas_call(correlate, out_shape=jax.ShapeDtypeStruct((over_tm, 2, own...  4.42 us

profile of v3, /device:TPU:16, one launch (start us, length us, event | category | flops | bytes accessed | tf_op | source)
XLA Modules:
  0.0 84.8 jit_solution(9070586200676513960)
XLA Ops:
  0.0 0.0 copy-start
  0.0 1.6 %copy-done = bf16[16,64,4,256]{3,2,1,0:T(4,128)(2,1)S(1)} copy-done((bf16[16,64,4,256]{3,2,1,0:T(4,128)(2,1)S(1)}, bf16[16,64,4,256]{3,2,1,0:T(4,128)(2,1)}, u32[]{:S(2)}) %copy-start) | copy-done | bytes 2097176
  1.6 0.7 pack.1
  2.3 0.0 copy-start.1
  2.3 0.0 copy-start.2
  2.3 0.0 copy-start.3
  2.3 0.0 copy-start.4
  2.3 0.0 copy-start.5
  2.3 0.0 copy-start.6
  2.3 0.0 copy-start.7
  2.3 0.0 copy-start.8
  2.4 62.9 %all_to_all.10.got_ref = bf16[32,16,2,8,128]{4,3,2,1,0:T(8,128)(2,1)S(1)} all-to-all(bf16[32,16,2,8,128]{4,3,2,1,0:T(8,128)(2,1)S(1)} %pack.1), channel_id=1, replica_groups=mesh['ap'=32,'tm'=8] {'ap'}, dimensions={0} | all-to-all | bytes 4194304 | tf_op jit(solution)/shard_map/all_to_all | solution.py:149
  65.3 0.0 copy-done.1
  65.3 0.0 copy-done.2
  65.3 0.0 copy-done.3
  65.3 0.0 copy-done.4
  65.3 0.0 copy-done.5
  65.3 0.0 copy-done.6
  65.3 0.0 copy-done.7
  65.3 0.0 copy-done.8
  65.3 4.4 %correlate.1 = bf16[8,2,2,32,256]{4,3,2,1,0:T(8,128)(2,1)S(1)} custom-call(bf16[32,16,2,8,128]{4,3,2,1,0:T(8,128)(2,1)S(1)} %all_to_all.10.got_ref, bf16[256,512]{1,0:T(8,128)(2,1)S(1)} %copy-done.4, bf16[512,256]{1,0:T(8,128)(2,1)S(1)} %copy-done.3, bf16[256,256]{1,0:T(8,128)(2,1)S(1)} %copy-done.7, bf16[256,256]{1,0:T(8,128)(2,1)S(1)} %copy-done.6, ...), custom_call_target="tpu_custom_call" | custom-call | tf_op jit(solution)/shard_map/correlate/pallas_call | solution.py:150
  69.8 14.2 %all_to_all.11 = bf16[8,2,2,32,256]{4,3,2,1,0:T(8,128)(2,1)S(1)} all-to-all(bf16[8,2,2,32,256]{4,3,2,1,0:T(8,128)(2,1)S(1)} %correlate.1), channel_id=1, replica_groups=mesh['ap'=32,'tm'=8] {'tm'}, dimensions={0} | all-to-all | bytes 1048576 | tf_op jit(solution)/shard_map/all_to_all | solution.py:159
  83.9 0.1 convert_reduce_fusion
  84.0 0.8 copy.12
Async XLA Ops:
  0.0 1.6 %copy-start = (bf16[16,64,4,256]{3,2,1,0:T(4,128)(2,1)S(1)}, bf16[16,64,4,256]{3,2,1,0:T(4,128)(2,1)}, u32[]{:S(2)}) copy-start(bf16[16,64,4,256]{3,2,1,0:T(4,128)(2,1)} %param.9) | copy-start | bytes 6291460
  2.3 63.0 %copy-start.1 = (bf16[256,512]{1,0:T(8,128)(2,1)S(1)}, bf16[256,512]{1,0:T(8,128)(2,1)}, u32[]{:S(2)}) copy-start(bf16[256,512]{1,0:T(8,128)(2,1)} %constant.23.clone.col_lo) | copy-start | bytes 786436
  2.3 63.0 %copy-start.2 = (bf16[256,512]{1,0:T(8,128)(2,1)S(1)}, bf16[256,512]{1,0:T(8,128)(2,1)}, u32[]{:S(2)}) copy-start(bf16[256,512]{1,0:T(8,128)(2,1)} %constant.22.clone.col_hi) | copy-start | bytes 786436
  2.3 63.0 %copy-start.3 = (bf16[512,256]{1,0:T(8,128)(2,1)S(1)}, bf16[512,256]{1,0:T(8,128)(2,1)}, u32[]{:S(2)}) copy-start(bf16[512,256]{1,0:T(8,128)(2,1)} %constant.19.clone.second_ref) | copy-start | bytes 786436
  2.3 63.0 %copy-start.4 = (bf16[256,512]{1,0:T(8,128)(2,1)S(1)}, bf16[256,512]{1,0:T(8,128)(2,1)}, u32[]{:S(2)}) copy-start(bf16[256,512]{1,0:T(8,128)(2,1)} %constant.18.clone.first_ref) | copy-start | bytes 786436
  2.3 63.0 %copy-start.5 = (f32[128,256]{1,0:T(8,128)S(1)}, f32[128,256]{1,0:T(8,128)}, u32[]{:S(2)}) copy-start(f32[128,256]{1,0:T(8,128)} %constant.24.clone.factor_ref) | copy-start | bytes 393220
  2.3 63.0 %copy-start.6 = (bf16[256,256]{1,0:T(8,128)(2,1)S(1)}, bf16[256,256]{1,0:T(8,128)(2,1)}, u32[]{:S(2)}) copy-start(bf16[256,256]{1,0:T(8,128)(2,1)} %constant.21.clone.row_lo) | copy-start | bytes 393220
  2.3 63.0 %copy-start.7 = (bf16[256,256]{1,0:T(8,128)(2,1)S(1)}, bf16[256,256]{1,0:T(8,128)(2,1)}, u32[]{:S(2)}) copy-start(bf16[256,256]{1,0:T(8,128)(2,1)} %constant.20.clone.row_hi) | copy-start | bytes 393220
  2.3 63.0 %copy-start.8 = (bf16[128,128]{1,0:T(8,128)(2,1)S(1)}, bf16[128,128]{1,0:T(8,128)(2,1)}, u32[]{:S(2)}) copy-start(bf16[128,128]{1,0:T(8,128)(2,1)} %constant.25.clone.flip_ref) | copy-start | bytes 98308

commit v4 on v3

--- a/solution.py
+++ b/solution.py
@@ -139,13 +139,13 @@
     view = view.transpose(0, 1, 2, 4, 3, 5).reshape(samples, over_ap, own, 2 * local_rows, grid_side)
     sent = pl.pallas_call(
         pack,
-        out_shape=jax.ShapeDtypeStruct((over_ap, samples) + view.shape[2:], BF16),
+        out_shape=pltpu.VMEM((over_ap, samples) + view.shape[2:], BF16),
         in_specs=[pl.BlockSpec(memory_space=pltpu.HBM)],
         out_specs=vmem,
         scratch_shapes=[pltpu.SemaphoreType.DMA((over_ap,))],
         compiler_params=params,
         name="pack",
-    )(view)
+    )(pltpu.with_memory_space_constraint(view, pltpu.HBM))
     got = lax.all_to_all(sent, "ap", 0, 0, tiled=True)
     terms = pl.pallas_call(
         correlate,

time: 85 us -> 84.6 us (level)
  local copies, waits for them, and re-layouts: 2.4 us -> 0.81 us
  Pallas kernels: 5.07 us -> 6.28 us
    unnamed x18 -> x16, local copies, waits for them, and re-layouts: 1.65 us -> 0.05 us
    pallas_call x1, Pallas kernels: 0.65 us -> 1.86 us  [shards(): pl.pallas_call(pack, out_shape=pltpu.VMEM((over_ap, samples) + view.shape...]
where the time goes in v4:
time: 84.6 us; the launch traced here: 84.4 us
  blocking collectives  77.1 us (91%)
  Pallas kernels  6.28 us (7%)
    all_to_all x1, blocking collectives, shards(): got = lax.all_to_all(sent, 'ap', 0, 0, tiled=True)  62.9 us
    all_to_all x1, blocking collectives, shards(): parts = lax.all_to_all(terms, 'tm', 0, 0, tiled=True)  14.2 us
    pallas_call x1, Pallas kernels, shards(): pl.pallas_call(correlate, out_shape=jax.ShapeDtypeStruct((over_tm, 2, own...  4.42 us
    pallas_call x1, Pallas kernels, shards(): pl.pallas_call(pack, out_shape=pltpu.VMEM((over_ap, samples) + view.shape...  1.86 us

profile of v4, /device:TPU:16, one launch (start us, length us, event | category | flops | bytes accessed | tf_op | source)
XLA Modules:
  0.0 84.4 jit_solution(8947999792094955978)
XLA Ops:
  0.0 1.9 %pack.1 = bf16[32,16,2,8,128]{4,3,2,1,0:T(8,128)(2,1)S(1)} custom-call(bf16[16,32,2,8,128]{4,3,2,1,0:T(8,128)(2,1)} %bitcast.6), custom_call_target="tpu_custom_call" | custom-call | tf_op jit(solution)/shard_map/pack/pallas_call | solution.py:140
  1.9 0.0 copy-start
  1.9 0.0 copy-start.1
  1.9 0.0 copy-start.2
  1.9 0.0 copy-start.3
  1.9 0.0 copy-start.4
  1.9 0.0 copy-start.5
  1.9 0.0 copy-start.6
  2.0 0.0 copy-start.7
  2.0 62.9 %all_to_all.10.got_ref = bf16[32,16,2,8,128]{4,3,2,1,0:T(8,128)(2,1)S(1)} all-to-all(bf16[32,16,2,8,128]{4,3,2,1,0:T(8,128)(2,1)S(1)} %pack.1), channel_id=1, replica_groups=mesh['ap'=32,'tm'=8] {'ap'}, dimensions={0} | all-to-all | bytes 4194304 | tf_op jit(solution)/shard_map/all_to_all | solution.py:149
  64.9 0.0 copy-done
  64.9 0.0 copy-done.1
  64.9 0.0 copy-done.2
  64.9 0.0 copy-done.3
  64.9 0.0 copy-done.4
  64.9 0.0 copy-done.5
  64.9 0.0 copy-done.6
  65.0 0.0 copy-done.7
  65.0 4.4 %correlate.1 = bf16[8,2,2,32,256]{4,3,2,1,0:T(8,128)(2,1)S(1)} custom-call(bf16[32,16,2,8,128]{4,3,2,1,0:T(8,128)(2,1)S(1)} %all_to_all.10.got_ref, bf16[256,512]{1,0:T(8,128)(2,1)S(1)} %copy-done.3, bf16[512,256]{1,0:T(8,128)(2,1)S(1)} %copy-done.2, bf16[256,256]{1,0:T(8,128)(2,1)S(1)} %copy-done.6, bf16[256,256]{1,0:T(8,128)(2,1)S(1)} %copy-done.5, ...), custom_call_target="tpu_custom_call" | custom-call | tf_op jit(solution)/shard_map/correlate/pallas_call | solution.py:150
  69.4 14.2 %all_to_all.11 = bf16[8,2,2,32,256]{4,3,2,1,0:T(8,128)(2,1)S(1)} all-to-all(bf16[8,2,2,32,256]{4,3,2,1,0:T(8,128)(2,1)S(1)} %correlate.1), channel_id=1, replica_groups=mesh['ap'=32,'tm'=8] {'tm'}, dimensions={0} | all-to-all | bytes 1048576 | tf_op jit(solution)/shard_map/all_to_all | solution.py:159
  83.6 0.1 convert_reduce_fusion
  83.6 0.8 copy.12
Async XLA Ops:
  1.9 63.0 %copy-start = (bf16[256,512]{1,0:T(8,128)(2,1)S(1)}, bf16[256,512]{1,0:T(8,128)(2,1)}, u32[]{:S(2)}) copy-start(bf16[256,512]{1,0:T(8,128)(2,1)} %constant.23.clone.col_lo) | copy-start | bytes 786436
  1.9 63.0 %copy-start.1 = (bf16[256,512]{1,0:T(8,128)(2,1)S(1)}, bf16[256,512]{1,0:T(8,128)(2,1)}, u32[]{:S(2)}) copy-start(bf16[256,512]{1,0:T(8,128)(2,1)} %constant.22.clone.col_hi) | copy-start | bytes 786436
  1.9 63.0 %copy-start.2 = (bf16[512,256]{1,0:T(8,128)(2,1)S(1)}, bf16[512,256]{1,0:T(8,128)(2,1)}, u32[]{:S(2)}) copy-start(bf16[512,256]{1,0:T(8,128)(2,1)} %constant.19.clone.second_ref) | copy-start | bytes 786436
  1.9 63.0 %copy-start.3 = (bf16[256,512]{1,0:T(8,128)(2,1)S(1)}, bf16[256,512]{1,0:T(8,128)(2,1)}, u32[]{:S(2)}) copy-start(bf16[256,512]{1,0:T(8,128)(2,1)} %constant.18.clone.first_ref) | copy-start | bytes 786436
  1.9 63.0 %copy-start.4 = (f32[128,256]{1,0:T(8,128)S(1)}, f32[128,256]{1,0:T(8,128)}, u32[]{:S(2)}) copy-start(f32[128,256]{1,0:T(8,128)} %constant.24.clone.factor_ref) | copy-start | bytes 393220
  1.9 63.0 %copy-start.5 = (bf16[256,256]{1,0:T(8,128)(2,1)S(1)}, bf16[256,256]{1,0:T(8,128)(2,1)}, u32[]{:S(2)}) copy-start(bf16[256,256]{1,0:T(8,128)(2,1)} %constant.21.clone.row_lo) | copy-start | bytes 393220
  1.9 63.0 %copy-start.6 = (bf16[256,256]{1,0:T(8,128)(2,1)S(1)}, bf16[256,256]{1,0:T(8,128)(2,1)}, u32[]{:S(2)}) copy-start(bf16[256,256]{1,0:T(8,128)(2,1)} %constant.20.clone.row_hi) | copy-start | bytes 393220
  2.0 63.0 %copy-start.7 = (bf16[128,128]{1,0:T(8,128)(2,1)S(1)}, bf16[128,128]{1,0:T(8,128)(2,1)}, u32[]{:S(2)}) copy-start(bf16[128,128]{1,0:T(8,128)(2,1)} %constant.25.clone.flip_ref) | copy-start | bytes 98308

commit v5 on v4

--- a/solution.py
+++ b/solution.py
@@ -66,8 +66,8 @@
         copy.wait()
 
 
-def rows_of(got_ref, t, c):
-    blocks = got_ref[:, t, c].astype(F32)
+def rows_of(got_ref, sample):
+    blocks = got_ref[(slice(None),) + sample].astype(F32)
     count, both, lanes = blocks.shape
     pairs = blocks.reshape(count // 2, 2, both, lanes)
     even, odd = pairs[:, 0], pairs[:, 1]
@@ -78,11 +78,11 @@
     return jnp.concatenate([real.reshape(rows, lanes), imag.reshape(rows, lanes)], 1).astype(BF16)
 
 
-def power_of(got_ref, first_ref, second_ref, c):
-    samples = got_ref.shape[1]
+def power_of(got_ref, first_ref, second_ref, part):
+    samples = got_ref.shape[2]
     pad = second_ref.shape[1]
     grid_side = pad // 2
-    rows = [rows_of(got_ref, t, c) for t in range(samples)]
+    rows = [rows_of(got_ref, (part, t)) for t in range(samples)]
     field = dot(jnp.concatenate(rows, 0), first_ref[...]).astype(BF16)
     total = None
     for t in range(samples):
@@ -96,33 +96,25 @@
 def correlate(
     got_ref, first_ref, second_ref, row_hi, row_lo, col_hi, col_lo, factor_ref, flip_ref, out_ref, power_ref
 ):
-    channels = got_ref.shape[2]
     pad = second_ref.shape[1]
     grid_side = pad // 2
-    owned = out_ref.shape[3]
+    owned = out_ref.shape[2]
     near = grid_side // owned
-    for c in range(channels):
-        power_ref[c] = power_of(got_ref, first_ref, second_ref, c)
-    powers = jnp.concatenate([power_ref[c] for c in range(channels)], 1)
-    half = dot3((row_hi[...], row_lo[...]), halves(powers))
-    half = jnp.concatenate([half[:, c * pad : (c + 1) * pad] for c in range(channels)], 0)
+    for part in range(got_ref.shape[1]):
+        power = power_of(got_ref, first_ref, second_ref, part)
+        power_ref[...] = power if part == 0 else power_ref[...] + power
+    half = dot3((row_hi[...], row_lo[...]), halves(power_ref[...]))
     both = dot3(halves(half), (col_hi[...], col_lo[...]))
-    mirrored = []
-    for c in range(channels):
-        one = both[c * pad : (c + 1) * pad]
-        cos_cos, cos_sin = one[:grid_side, :pad], one[:grid_side, pad:]
-        sin_cos, sin_sin = one[grid_side:, :pad], one[grid_side:, pad:]
-        plus = (cos_cos - sin_sin, cos_sin + sin_cos)
-        minus = (cos_cos + sin_sin, cos_sin - sin_cos)
-        for part in range(2):
-            lower = (plus[part] * factor_ref[...]).astype(BF16)
-            out_ref[:near, part, c] = lower.reshape(near, owned, pad)
-            mirrored.append((minus[part] * factor_ref[...]).astype(BF16))
+    cos_cos, cos_sin = both[:grid_side, :pad], both[:grid_side, pad:]
+    sin_cos, sin_sin = both[grid_side:, :pad], both[grid_side:, pad:]
+    plus = (cos_cos - sin_sin, cos_sin + sin_cos)
+    minus = (cos_cos + sin_sin, cos_sin - sin_cos)
+    mirrored = [(m * factor_ref[...]).astype(BF16) for m in minus]
     upper = dot(flip_ref[...], jnp.concatenate(mirrored, 1)).astype(BF16)
-    for c in range(channels):
-        for part in range(2):
-            at = (2 * c + part) * pad
-            out_ref[near:, part, c] = upper[:, at : at + pad].reshape(near, owned, pad)
+    for part in range(2):
+        lower = (plus[part] * factor_ref[...]).astype(BF16)
+        out_ref[:near, part] = lower.reshape(near, owned, pad)
+        out_ref[near:, part] = upper[:, part * pad : (part + 1) * pad].reshape(near, owned, pad)
 
 
 def shards(voltages):
@@ -135,29 +127,35 @@
     consts = tables(grid_side, pad_side, samples * over_tm)
     vmem = pl.BlockSpec(memory_space=pltpu.VMEM)
     params = pltpu.CompilerParams(vmem_limit_bytes=VMEM_BYTES)
-    view = voltages.reshape(samples, over_ap, own, local_rows, 2, grid_side)
-    view = view.transpose(0, 1, 2, 4, 3, 5).reshape(samples, over_ap, own, 2 * local_rows, grid_side)
+    view = voltages.reshape(samples, channels, local_rows, 2, grid_side)
+    view = view.transpose(0, 1, 3, 2, 4).reshape(samples, channels, 2 * local_rows, grid_side)
     sent = pl.pallas_call(
         pack,
-        out_shape=pltpu.VMEM((over_ap, samples) + view.shape[2:], BF16),
+        out_shape=pltpu.VMEM((channels, samples) + view.shape[2:], BF16),
         in_specs=[pl.BlockSpec(memory_space=pltpu.HBM)],
         out_specs=vmem,
-        scratch_shapes=[pltpu.SemaphoreType.DMA((over_ap,))],
+        scratch_shapes=[pltpu.SemaphoreType.DMA((channels,))],
         compiler_params=params,
         name="pack",
     )(pltpu.with_memory_space_constraint(view, pltpu.HBM))
-    got = lax.all_to_all(sent, "ap", 0, 0, tiled=True)
+    groups = [
+        [t * over_ap + a for a in range(over_ap) for t in range(run, run + own)]
+        for run in range(0, over_tm, own)
+    ]
+    got = lax.all_to_all(sent, ("tm", "ap"), 0, 0, axis_index_groups=groups, tiled=True)
+    got = got.reshape((over_ap, own) + got.shape[1:])
     terms = pl.pallas_call(
         correlate,
-        out_shape=jax.ShapeDtypeStruct((over_tm, 2, own, owned, pad_side), BF16),
+        out_shape=jax.ShapeDtypeStruct((over_tm, 2, owned, pad_side), BF16),
         in_specs=[vmem] * (1 + len(consts)),
         out_specs=vmem,
-        scratch_shapes=[pltpu.VMEM((own, pad_side, pad_side), F32)],
+        scratch_shapes=[pltpu.VMEM((pad_side, pad_side), F32)],
         compiler_params=params,
         name="correlate",
     )(got, *[jnp.asarray(c) for c in consts])
     parts = lax.all_to_all(terms, "tm", 0, 0, tiled=True)
-    return jnp.sum(parts.astype(F32), axis=0).transpose(2, 0, 1, 3)
+    parts = parts.reshape((over_tm // own, own) + parts.shape[1:])
+    return jnp.sum(parts.astype(F32), axis=0).transpose(2, 1, 0, 3)
 
 
 def solution(mesh):

time: 84.6 us -> 82.9 us (0.980)
  blocking collectives: 77.1 us -> 74.8 us
    all_to_all x1, blocking collectives: 14.2 us -> 11.6 us  [shards(): parts = lax.all_to_all(terms, 'tm', 0, 0, tiled=True)]
where the time goes in v5:
time: 82.9 us; the launch traced here: 82.5 us
  blocking collectives  74.8 us (90%)
  Pallas kernels  6.72 us (8%)
    all_to_all x1, blocking collectives, shards(): lax.all_to_all(sent, ('tm', 'ap'), 0, 0, axis_index_groups=groups, tiled=...  63.2 us
    all_to_all x1, blocking collectives, shards(): parts = lax.all_to_all(terms, 'tm', 0, 0, tiled=True)  11.6 us
    pallas_call x1, Pallas kernels, shards(): pl.pallas_call(correlate, out_shape=jax.ShapeDtypeStruct((over_tm, 2, own...  4.61 us
    pallas_call x1, Pallas kernels, shards(): pl.pallas_call(pack, out_shape=pltpu.VMEM((channels, samples) + view.shap...  2.1 us

profile of v5, /device:TPU:16, one launch (start us, length us, event | category | flops | bytes accessed | tf_op | source)
XLA Modules:
  0.0 82.5 jit_solution(7710535500162314383)
XLA Ops:
  0.0 2.1 %pack.1 = bf16[64,16,8,128]{3,2,1,0:T(8,128)(2,1)S(1)} custom-call(bf16[16,64,8,128]{3,2,1,0:T(8,128)(2,1)} %bitcast.10), custom_call_target="tpu_custom_call" | custom-call | tf_op jit(solution)/shard_map/pack/pallas_call | solution.py:132
  2.1 0.0 copy-start
  2.1 0.0 copy-start.1
  2.1 0.0 copy-start.2
  2.1 0.0 copy-start.3
  2.2 0.0 copy-start.4
  2.2 0.0 copy-start.5
  2.2 0.0 copy-start.6
  2.2 0.0 copy-start.7
  2.2 63.2 %all_to_all.10 = bf16[64,16,8,128]{3,2,1,0:T(8,128)(2,1)S(1)} all-to-all(bf16[64,16,8,128]{3,2,1,0:T(8,128)(2,1)S(1)} %pack.1), channel_id=1, replica_groups={{0,1,8,9,16,17,24,25,32,33,40,41,48,49,56,57,64,65,72,73,80,81,88,89,96..., dimensions={0} | all-to-all | bytes 4194304 | tf_op jit(solution)/shard_map/all_to_all | solution.py:145
  65.4 0.0 copy-done
  65.4 0.0 copy-done.1
  65.4 0.0 copy-done.2
  65.4 0.0 copy-done.3
  65.4 0.0 copy-done.4
  65.4 0.0 copy-done.5
  65.4 0.0 copy-done.6
  65.5 0.0 copy-done.7
  65.5 4.6 %correlate.1 = bf16[8,2,32,256]{3,2,1,0:T(8,128)(2,1)S(1)} custom-call(bf16[32,2,16,8,128]{4,3,2,1,0:T(8,128)(2,1)S(1)} %bitcast.9, bf16[256,512]{1,0:T(8,128)(2,1)S(1)} %copy-done.3, bf16[512,256]{1,0:T(8,128)(2,1)S(1)} %copy-done.2, bf16[256,256]{1,0:T(8,128)(2,1)S(1)} %copy-done.6, bf16[256,256]{1,0:T(8,128)(2,1)S(1)} %copy-done.5, ...), custom_call_target="tpu_custom_call" | custom-call | tf_op jit(solution)/shard_map/correlate/pallas_call | solution.py:147
  70.1 11.6 %all_to_all.11 = bf16[8,2,32,256]{3,2,1,0:T(8,128)(2,1)S(1)} all-to-all(bf16[8,2,32,256]{3,2,1,0:T(8,128)(2,1)S(1)} %correlate.1), channel_id=1, replica_groups=mesh['ap'=32,'tm'=8] {'tm'}, dimensions={0} | all-to-all | bytes 524288 | tf_op jit(solution)/shard_map/all_to_all | solution.py:156
  81.8 0.8 copy.12
  (1 shorter events, 0.0 us)
Async XLA Ops:
  2.1 63.3 %copy-start = (bf16[256,512]{1,0:T(8,128)(2,1)S(1)}, bf16[256,512]{1,0:T(8,128)(2,1)}, u32[]{:S(2)}) copy-start(bf16[256,512]{1,0:T(8,128)(2,1)} %constant.23.clone.col_lo) | copy-start | bytes 786436
  2.1 63.3 %copy-start.1 = (bf16[256,512]{1,0:T(8,128)(2,1)S(1)}, bf16[256,512]{1,0:T(8,128)(2,1)}, u32[]{:S(2)}) copy-start(bf16[256,512]{1,0:T(8,128)(2,1)} %constant.22.clone.col_hi) | copy-start | bytes 786436
  2.1 63.3 %copy-start.2 = (bf16[512,256]{1,0:T(8,128)(2,1)S(1)}, bf16[512,256]{1,0:T(8,128)(2,1)}, u32[]{:S(2)}) copy-start(bf16[512,256]{1,0:T(8,128)(2,1)} %constant.19.clone.second_ref) | copy-start | bytes 786436
  2.1 63.3 %copy-start.3 = (bf16[256,512]{1,0:T(8,128)(2,1)S(1)}, bf16[256,512]{1,0:T(8,128)(2,1)}, u32[]{:S(2)}) copy-start(bf16[256,512]{1,0:T(8,128)(2,1)} %constant.18.clone.first_ref) | copy-start | bytes 786436
  2.2 63.3 %copy-start.4 = (f32[128,256]{1,0:T(8,128)S(1)}, f32[128,256]{1,0:T(8,128)}, u32[]{:S(2)}) copy-start(f32[128,256]{1,0:T(8,128)} %constant.24.clone.factor_ref) | copy-start | bytes 393220
  2.2 63.3 %copy-start.5 = (bf16[256,256]{1,0:T(8,128)(2,1)S(1)}, bf16[256,256]{1,0:T(8,128)(2,1)}, u32[]{:S(2)}) copy-start(bf16[256,256]{1,0:T(8,128)(2,1)} %constant.21.clone.row_lo) | copy-start | bytes 393220
  2.2 63.3 %copy-start.6 = (bf16[256,256]{1,0:T(8,128)(2,1)S(1)}, bf16[256,256]{1,0:T(8,128)(2,1)}, u32[]{:S(2)}) copy-start(bf16[256,256]{1,0:T(8,128)(2,1)} %constant.20.clone.row_hi) | copy-start | bytes 393220
  2.2 63.3 %copy-start.7 = (bf16[128,128]{1,0:T(8,128)(2,1)S(1)}, bf16[128,128]{1,0:T(8,128)(2,1)}, u32[]{:S(2)}) copy-start(bf16[128,128]{1,0:T(8,128)(2,1)} %constant.25.clone.flip_ref) | copy-start | bytes 98308

commit v6 on v5

--- a/solution.py
+++ b/solution.py
@@ -1,3 +1,4 @@
+import functools
 import math
 
 import jax
@@ -11,6 +12,12 @@
 F32 = jnp.float32
 BF16 = jnp.bfloat16
 VMEM_BYTES = 48 * 1024 * 1024
+ORDER = (
+    46, 20, 15, 26, 49, 35, 61, 0, 12, 56, 53, 18, 41, 7, 27, 38,
+    30, 19, 33, 63, 10, 48, 45, 4, 37, 11, 25, 55, 2, 22, 40, 60,
+    47, 3, 29, 32, 17, 52, 14, 58, 59, 6, 21, 39, 9, 24, 44, 50,
+    13, 42, 31, 1, 62, 51, 36, 16, 28, 57, 8, 23, 54, 43, 34, 5,
+)
 
 
 def angles(rows, cols, pad_side):
@@ -29,9 +36,11 @@
     cosine, sine = np.cos(padded), np.sin(padded)
     first = np.block([[cosine, -sine], [sine, cosine]]).astype(BF16)
     second = np.block([[cosine.T, sine.T], [-sine.T, cosine.T]]).astype(BF16)
-    by_row = split(np.concatenate([cosine, sine], 0))
+    high, low = split(np.concatenate([cosine, sine], 0))
+    by_row = np.concatenate([high, high, low], 1)
     whole = angles(index, index, pad_side)
-    by_col = split(np.concatenate([np.cos(whole), np.sin(whole)], 1))
+    high, low = split(np.concatenate([np.cos(whole), np.sin(whole)], 1))
+    by_col = np.concatenate([high, low, high], 0)
     signed = np.where(index < grid_side, index, index - pad_side)
     pairs = np.maximum(grid_side - np.abs(signed), 0)
     count = pairs[:, None] * pairs[None, :]
@@ -39,7 +48,7 @@
     scale = 1.0 / (float(pad_side * pad_side) * np.sqrt(np.maximum(count, 1) * float(samples)))
     factor = np.where(keep, scale, 0.0).astype(np.float32)[:grid_side]
     flip = (dishes[:, None] + dishes[None, :] == grid_side).astype(BF16)
-    return first, second, *by_row, *by_col, factor, flip
+    return first, second, by_row, by_col, factor, flip
 
 
 def dot(a, b):
@@ -51,14 +60,10 @@
     return high, (value - high.astype(F32)).astype(BF16)
 
 
-def dot3(a, b):
-    return dot(a[0], b[0]) + (dot(a[0], b[1]) + dot(a[1], b[0]))
-
-
-def pack(x_ref, out_ref, sems):
+def pack(order, x_ref, out_ref, sems):
     copies = [
-        pltpu.make_async_copy(x_ref.at[:, d], out_ref.at[d], sems.at[d])
-        for d in range(out_ref.shape[0])
+        pltpu.make_async_copy(x_ref.at[:, channel], out_ref.at[slot], sems.at[slot])
+        for slot, channel in enumerate(order)
     ]
     for copy in copies:
         copy.start()
@@ -66,23 +71,22 @@
         copy.wait()
 
 
-def rows_of(got_ref, sample):
-    blocks = got_ref[(slice(None),) + sample].astype(F32)
-    count, both, lanes = blocks.shape
-    pairs = blocks.reshape(count // 2, 2, both, lanes)
-    even, odd = pairs[:, 0], pairs[:, 1]
+def rows_of(got_ref, slots, t):
+    even = jnp.stack([got_ref[slot, t].astype(F32) for slot in slots[0::2]])
+    odd = jnp.stack([got_ref[slot, t].astype(F32) for slot in slots[1::2]])
+    count, both, lanes = even.shape
     upper = lax.broadcasted_iota(jnp.int32, even.shape, 1) < both // 2
     real = jnp.where(upper, even, pltpu.roll(odd, both // 2, 1))
     imag = jnp.where(upper, pltpu.roll(even, both // 2, 1), odd)
-    rows = count * both // 2
+    rows = count * both
     return jnp.concatenate([real.reshape(rows, lanes), imag.reshape(rows, lanes)], 1).astype(BF16)
 
 
-def power_of(got_ref, first_ref, second_ref, part):
-    samples = got_ref.shape[2]
+def power_of(got_ref, first_ref, second_ref, slots):
+    samples = got_ref.shape[1]
     pad = second_ref.shape[1]
     grid_side = pad // 2
-    rows = [rows_of(got_ref, (part, t)) for t in range(samples)]
+    rows = [rows_of(got_ref, slots, t) for t in range(samples)]
     field = dot(jnp.concatenate(rows, 0), first_ref[...]).astype(BF16)
     total = None
     for t in range(samples):
@@ -93,18 +97,18 @@
     return total
 
 
-def correlate(
-    got_ref, first_ref, second_ref, row_hi, row_lo, col_hi, col_lo, factor_ref, flip_ref, out_ref, power_ref
-):
+def correlate(slots, got_ref, first_ref, second_ref, by_row, by_col, factor_ref, flip_ref, out_ref, power_ref):
     pad = second_ref.shape[1]
     grid_side = pad // 2
     owned = out_ref.shape[2]
     near = grid_side // owned
-    for part in range(got_ref.shape[1]):
-        power = power_of(got_ref, first_ref, second_ref, part)
+    for part, places in enumerate(slots):
+        power = power_of(got_ref, first_ref, second_ref, places)
         power_ref[...] = power if part == 0 else power_ref[...] + power
-    half = dot3((row_hi[...], row_lo[...]), halves(power_ref[...]))
-    both = dot3(halves(half), (col_hi[...], col_lo[...]))
+    high, low = halves(power_ref[...])
+    half = dot(by_row[...], jnp.concatenate([high, low, high], 0))
+    high, low = halves(half)
+    both = dot(jnp.concatenate([high, high, low], 1), by_col[...])
     cos_cos, cos_sin = both[:grid_side, :pad], both[:grid_side, pad:]
     sin_cos, sin_sin = both[grid_side:, :pad], both[grid_side:, pad:]
     plus = (cos_cos - sin_sin, cos_sin + sin_cos)
@@ -129,8 +133,9 @@
     params = pltpu.CompilerParams(vmem_limit_bytes=VMEM_BYTES)
     view = voltages.reshape(samples, channels, local_rows, 2, grid_side)
     view = view.transpose(0, 1, 3, 2, 4).reshape(samples, channels, 2 * local_rows, grid_side)
+    order = ORDER if len(ORDER) == channels else tuple(range(channels))
     sent = pl.pallas_call(
-        pack,
+        functools.partial(pack, order),
         out_shape=pltpu.VMEM((channels, samples) + view.shape[2:], BF16),
         in_specs=[pl.BlockSpec(memory_space=pltpu.HBM)],
         out_specs=vmem,
@@ -139,13 +144,13 @@
         name="pack",
     )(pltpu.with_memory_space_constraint(view, pltpu.HBM))
     groups = [
-        [t * over_ap + a for a in range(over_ap) for t in range(run, run + own)]
+        [(run + channel % own) * over_ap + channel // own for channel in order]
         for run in range(0, over_tm, own)
     ]
+    slots = [[order.index(a * own + p) for a in range(over_ap)] for p in range(own)]
     got = lax.all_to_all(sent, ("tm", "ap"), 0, 0, axis_index_groups=groups, tiled=True)
-    got = got.reshape((over_ap, own) + got.shape[1:])
     terms = pl.pallas_call(
-        correlate,
+        functools.partial(correlate, slots),
         out_shape=jax.ShapeDtypeStruct((over_tm, 2, owned, pad_side), BF16),
         in_specs=[vmem] * (1 + len(consts)),
         out_specs=vmem,

time: 82.9 us -> 79.2 us (0.955)
  blocking collectives: 74.8 us -> 71.5 us
    all_to_all x1, blocking collectives: 63.2 us -> 60.1 us  [shards(): lax.all_to_all(sent, ('tm', 'ap'), 0, 0, axis_index_groups=groups, tiled=...]
where the time goes in v6:
time: 79.2 us; the launch traced here: 78.9 us
  blocking collectives  71.5 us (90%)
  Pallas kernels  6.46 us (8%)
  local copies, waits for them, and re-layouts  0.8 us (1%)
    all_to_all x1, blocking collectives, shards(): lax.all_to_all(sent, ('tm', 'ap'), 0, 0, axis_index_groups=groups, tiled=...  60.1 us
    all_to_all x1, blocking collectives, shards(): parts = lax.all_to_all(terms, 'tm', 0, 0, tiled=True)  11.4 us
    pallas_call x1, Pallas kernels, shards(): pl.pallas_call(functools.partial(correlate, slots), out_shape=jax.ShapeDt...  4.36 us
    pallas_call x1, Pallas kernels, shards(): pl.pallas_call(functools.partial(pack, order), out_shape=pltpu.VMEM((chan...  2.1 us

profile of v6, /device:TPU:16, one launch (start us, length us, event | category | flops | bytes accessed | tf_op | source)
XLA Modules:
  0.0 78.9 jit_solution(17769313143442022709)
XLA Ops:
  0.0 2.1 %pack.1 = bf16[64,16,8,128]{3,2,1,0:T(8,128)(2,1)S(1)} custom-call(bf16[16,64,8,128]{3,2,1,0:T(8,128)(2,1)} %bitcast.8), custom_call_target="tpu_custom_call" | custom-call | tf_op jit(solution)/shard_map/pack/pallas_call | solution.py:137
  2.1 0.0 copy-start
  2.1 0.0 copy-start.1
  2.1 0.0 copy-start.2
  2.1 0.0 copy-start.3
  2.2 0.0 copy-start.4
  2.2 0.0 copy-start.5
  2.2 60.1 %all_to_all.10.got_ref = bf16[64,16,8,128]{3,2,1,0:T(8,128)(2,1)S(1)} all-to-all(bf16[64,16,8,128]{3,2,1,0:T(8,128)(2,1)S(1)} %pack.1), channel_id=1, replica_groups={{184,80,57,104,193,137,241,0,48,224,209,72,161,25,105,152,120,73,129,24..., dimensions={0} | all-to-all | bytes 4194304 | tf_op jit(solution)/shard_map/all_to_all | solution.py:151
  62.3 0.0 copy-done
  62.3 0.0 copy-done.1
  62.3 0.0 copy-done.2
  62.3 0.0 copy-done.3
  62.3 0.0 copy-done.4
  62.3 0.0 copy-done.5
  62.3 4.4 %correlate.1 = bf16[8,2,32,256]{3,2,1,0:T(8,128)(2,1)S(1)} custom-call(bf16[64,16,8,128]{3,2,1,0:T(8,128)(2,1)S(1)} %all_to_all.10.got_ref, bf16[256,512]{1,0:T(8,128)(2,1)S(1)} %copy-done.3, bf16[512,256]{1,0:T(8,128)(2,1)S(1)} %copy-done.2, bf16[256,768]{1,0:T(8,128)(2,1)S(1)} %copy-done.1, bf16[768,512]{1,0:T(8,128)(2,1)S(1)} %copy-done, ...), custom_call_target="tpu_custom_call" | custom-call | tf_op jit(solution)/shard_map/correlate/pallas_call | solution.py:152
  66.7 11.4 %all_to_all.11 = bf16[8,2,32,256]{3,2,1,0:T(8,128)(2,1)S(1)} all-to-all(bf16[8,2,32,256]{3,2,1,0:T(8,128)(2,1)S(1)} %correlate.1), channel_id=1, replica_groups=mesh['ap'=32,'tm'=8] {'tm'}, dimensions={0} | all-to-all | bytes 524288 | tf_op jit(solution)/shard_map/all_to_all | solution.py:161
  78.2 0.8 copy.10
  (1 shorter events, 0.0 us)
Async XLA Ops:
  2.1 60.2 %copy-start = (bf16[768,512]{1,0:T(8,128)(2,1)S(1)}, bf16[768,512]{1,0:T(8,128)(2,1)}, u32[]{:S(2)}) copy-start(bf16[768,512]{1,0:T(8,128)(2,1)} %constant.17.clone.by_col) | copy-start | bytes 2359300
  2.1 60.2 %copy-start.1 = (bf16[256,768]{1,0:T(8,128)(2,1)S(1)}, bf16[256,768]{1,0:T(8,128)(2,1)}, u32[]{:S(2)}) copy-start(bf16[256,768]{1,0:T(8,128)(2,1)} %constant.16.clone.by_row) | copy-start | bytes 1179652
  2.1 60.1 %copy-start.2 = (bf16[512,256]{1,0:T(8,128)(2,1)S(1)}, bf16[512,256]{1,0:T(8,128)(2,1)}, u32[]{:S(2)}) copy-start(bf16[512,256]{1,0:T(8,128)(2,1)} %constant.15.clone.second_ref) | copy-start | bytes 786436
  2.1 60.1 %copy-start.3 = (bf16[256,512]{1,0:T(8,128)(2,1)S(1)}, bf16[256,512]{1,0:T(8,128)(2,1)}, u32[]{:S(2)}) copy-start(bf16[256,512]{1,0:T(8,128)(2,1)} %constant.14.clone.first_ref) | copy-start | bytes 786436
  2.2 60.1 %copy-start.4 = (f32[128,256]{1,0:T(8,128)S(1)}, f32[128,256]{1,0:T(8,128)}, u32[]{:S(2)}) copy-start(f32[128,256]{1,0:T(8,128)} %constant.18.clone.factor_ref) | copy-start | bytes 393220
  2.2 60.1 %copy-start.5 = (bf16[128,128]{1,0:T(8,128)(2,1)S(1)}, bf16[128,128]{1,0:T(8,128)(2,1)}, u32[]{:S(2)}) copy-start(bf16[128,128]{1,0:T(8,128)(2,1)} %constant.19.clone.flip_ref) | copy-start | bytes 98308

commit v7 on v6

--- a/solution.py
+++ b/solution.py
@@ -13,11 +13,12 @@
 BF16 = jnp.bfloat16
 VMEM_BYTES = 48 * 1024 * 1024
 ORDER = (
-    46, 20, 15, 26, 49, 35, 61, 0, 12, 56, 53, 18, 41, 7, 27, 38,
-    30, 19, 33, 63, 10, 48, 45, 4, 37, 11, 25, 55, 2, 22, 40, 60,
-    47, 3, 29, 32, 17, 52, 14, 58, 59, 6, 21, 39, 9, 24, 44, 50,
-    13, 42, 31, 1, 62, 51, 36, 16, 28, 57, 8, 23, 54, 43, 34, 5,
+    46, 20, 15, 26, 49, 35, 61, 0, 12, 56, 53, 18, 41, 7, 27, 34,
+    43, 54, 23, 8, 57, 28, 16, 36, 51, 62, 1, 31, 42, 13, 50, 44,
+    24, 9, 39, 21, 6, 59, 58, 14, 55, 22, 40, 60, 47, 3, 29, 32,
+    17, 52, 2, 25, 11, 37, 4, 45, 48, 10, 63, 33, 19, 30, 38, 5,
 )
+LAST_ORDER = (4, 1, 6, 2, 3, 7, 5, 0)
 
 
 def angles(rows, cols, pad_side):
@@ -97,13 +98,13 @@
     return total
 
 
-def correlate(slots, got_ref, first_ref, second_ref, by_row, by_col, factor_ref, flip_ref, out_ref, power_ref):
+def correlate(slots, places, got_ref, first_ref, second_ref, by_row, by_col, factor_ref, flip_ref, out_ref, power_ref):
     pad = second_ref.shape[1]
     grid_side = pad // 2
     owned = out_ref.shape[2]
     near = grid_side // owned
-    for part, places in enumerate(slots):
-        power = power_of(got_ref, first_ref, second_ref, places)
+    for part, senders in enumerate(slots):
+        power = power_of(got_ref, first_ref, second_ref, senders)
         power_ref[...] = power if part == 0 else power_ref[...] + power
     high, low = halves(power_ref[...])
     half = dot(by_row[...], jnp.concatenate([high, low, high], 0))
@@ -117,8 +118,9 @@
     upper = dot(flip_ref[...], jnp.concatenate(mirrored, 1)).astype(BF16)
     for part in range(2):
         lower = (plus[part] * factor_ref[...]).astype(BF16)
-        out_ref[:near, part] = lower.reshape(near, owned, pad)
-        out_ref[near:, part] = upper[:, part * pad : (part + 1) * pad].reshape(near, owned, pad)
+        for i in range(near):
+            out_ref[places[i], part] = lower[i * owned : (i + 1) * owned]
+            out_ref[places[near + i], part] = upper[i * owned : (i + 1) * owned, part * pad : (part + 1) * pad]
 
 
 def shards(voltages):
@@ -149,8 +151,9 @@
     ]
     slots = [[order.index(a * own + p) for a in range(over_ap)] for p in range(own)]
     got = lax.all_to_all(sent, ("tm", "ap"), 0, 0, axis_index_groups=groups, tiled=True)
+    last = LAST_ORDER if len(LAST_ORDER) == over_tm else tuple(range(over_tm))
     terms = pl.pallas_call(
-        functools.partial(correlate, slots),
+        functools.partial(correlate, slots, [last.index(t) for t in range(over_tm)]),
         out_shape=jax.ShapeDtypeStruct((over_tm, 2, owned, pad_side), BF16),
         in_specs=[vmem] * (1 + len(consts)),
         out_specs=vmem,
@@ -158,9 +161,11 @@
         compiler_params=params,
         name="correlate",
     )(got, *[jnp.asarray(c) for c in consts])
-    parts = lax.all_to_all(terms, "tm", 0, 0, tiled=True)
-    parts = parts.reshape((over_tm // own, own) + parts.shape[1:])
-    return jnp.sum(parts.astype(F32), axis=0).transpose(2, 1, 0, 3)
+    parts = lax.all_to_all(terms, "tm", 0, 0, axis_index_groups=[list(last)], tiled=True)
+    sums = [
+        sum(parts[i].astype(F32) for i, t in enumerate(last) if t % own == p) for p in range(own)
+    ]
+    return jnp.stack(sums, 0).transpose(2, 1, 0, 3)
 
 
 def solution(mesh):

time: 79.2 us -> 77.4 us (0.977)
  blocking collectives: 71.5 us -> 69.5 us
    all_to_all x1, blocking collectives: 11.4 us -> 9.76 us  [shards(): lax.all_to_all(terms, 'tm', 0, 0, axis_index_groups=[list(last)], tiled=T...]
where the time goes in v7:
time: 77.4 us; the launch traced here: 76.9 us
  blocking collectives  69.5 us (90%)
  Pallas kernels  6.45 us (8%)
  local copies, waits for them, and re-layouts  0.8 us (1%)
    all_to_all x1, blocking collectives, shards(): lax.all_to_all(sent, ('tm', 'ap'), 0, 0, axis_index_groups=groups, tiled=...  59.8 us
    all_to_all x1, blocking collectives, shards(): lax.all_to_all(terms, 'tm', 0, 0, axis_index_groups=[list(last)], tiled=T...  9.76 us
    pallas_call x1, Pallas kernels, shards(): pl.pallas_call(functools.partial(correlate, slots, [last.index(t) for t i...  4.35 us
    pallas_call x1, Pallas kernels, shards(): pl.pallas_call(functools.partial(pack, order), out_shape=pltpu.VMEM((chan...  2.1 us

profile of v7, /device:TPU:16, one launch (start us, length us, event | category | flops | bytes accessed | tf_op | source)
XLA Modules:
  0.0 76.9 jit_solution(14130858389467958275)
XLA Ops:
  0.0 2.1 %pack.1 = bf16[64,16,8,128]{3,2,1,0:T(8,128)(2,1)S(1)} custom-call(bf16[16,64,8,128]{3,2,1,0:T(8,128)(2,1)} %bitcast.7), custom_call_target="tpu_custom_call" | custom-call | tf_op jit(solution)/shard_map/pack/pallas_call | solution.py:139
  2.1 0.0 copy-start
  2.1 0.0 copy-start.1
  2.1 0.0 copy-start.2
  2.1 0.0 copy-start.3
  2.2 0.0 copy-start.4
  2.2 0.0 copy-start.5
  2.2 59.8 %all_to_all.10.got_ref = bf16[64,16,8,128]{3,2,1,0:T(8,128)(2,1)S(1)} all-to-all(bf16[64,16,8,128]{3,2,1,0:T(8,128)(2,1)S(1)} %pack.1), channel_id=1, replica_groups={{184,80,57,104,193,137,241,0,48,224,209,72,161,25,105,136,169,216,89,32..., dimensions={0} | all-to-all | bytes 4194304 | tf_op jit(solution)/shard_map/all_to_all | solution.py:153
  61.9 0.0 copy-done
  62.0 0.0 copy-done.1
  62.0 0.0 copy-done.2
  62.0 0.0 copy-done.3
  62.0 0.0 copy-done.4
  62.0 0.0 copy-done.5
  62.0 4.4 %correlate.1 = bf16[8,2,32,256]{3,2,1,0:T(8,128)(2,1)S(1)} custom-call(bf16[64,16,8,128]{3,2,1,0:T(8,128)(2,1)S(1)} %all_to_all.10.got_ref, bf16[256,512]{1,0:T(8,128)(2,1)S(1)} %copy-done.3, bf16[512,256]{1,0:T(8,128)(2,1)S(1)} %copy-done.2, bf16[256,768]{1,0:T(8,128)(2,1)S(1)} %copy-done.1, bf16[768,512]{1,0:T(8,128)(2,1)S(1)} %copy-done, ...), custom_call_target="tpu_custom_call" | custom-call | tf_op jit(solution)/shard_map/correlate/pallas_call | solution.py:155
  66.3 9.8 %all_to_all.11 = bf16[8,2,32,256]{3,2,1,0:T(8,128)(2,1)S(1)} all-to-all(bf16[8,2,32,256]{3,2,1,0:T(8,128)(2,1)S(1)} %correlate.1), channel_id=1, replica_groups={{4,1,6,2,3,7,5,0},{12,9,14,10,11,15,13,8},{20,17,22,18,19,23,21,16},{28..., dimensions={0} | all-to-all | bytes 524288 | tf_op jit(solution)/shard_map/all_to_all | solution.py:164
  76.2 0.8 copy.9
  (2 shorter events, 0.0 us)
Async XLA Ops:
  2.1 59.8 %copy-start = (bf16[768,512]{1,0:T(8,128)(2,1)S(1)}, bf16[768,512]{1,0:T(8,128)(2,1)}, u32[]{:S(2)}) copy-start(bf16[768,512]{1,0:T(8,128)(2,1)} %constant.15.clone.by_col) | copy-start | bytes 2359300
  2.1 59.8 %copy-start.1 = (bf16[256,768]{1,0:T(8,128)(2,1)S(1)}, bf16[256,768]{1,0:T(8,128)(2,1)}, u32[]{:S(2)}) copy-start(bf16[256,768]{1,0:T(8,128)(2,1)} %constant.14.clone.by_row) | copy-start | bytes 1179652
  2.1 59.8 %copy-start.2 = (bf16[512,256]{1,0:T(8,128)(2,1)S(1)}, bf16[512,256]{1,0:T(8,128)(2,1)}, u32[]{:S(2)}) copy-start(bf16[512,256]{1,0:T(8,128)(2,1)} %constant.13.clone.second_ref) | copy-start | bytes 786436
  2.1 59.8 %copy-start.3 = (bf16[256,512]{1,0:T(8,128)(2,1)S(1)}, bf16[256,512]{1,0:T(8,128)(2,1)}, u32[]{:S(2)}) copy-start(bf16[256,512]{1,0:T(8,128)(2,1)} %constant.12.clone.first_ref) | copy-start | bytes 786436
  2.2 59.8 %copy-start.4 = (f32[128,256]{1,0:T(8,128)S(1)}, f32[128,256]{1,0:T(8,128)}, u32[]{:S(2)}) copy-start(f32[128,256]{1,0:T(8,128)} %constant.16.clone.factor_ref) | copy-start | bytes 393220
  2.2 59.8 %copy-start.5 = (bf16[128,128]{1,0:T(8,128)(2,1)S(1)}, bf16[128,128]{1,0:T(8,128)(2,1)}, u32[]{:S(2)}) copy-start(bf16[128,128]{1,0:T(8,128)(2,1)} %constant.17.clone.flip_ref) | copy-start | bytes 98308

commit v8 on v7

--- a/solution.py
+++ b/solution.py
@@ -13,10 +13,10 @@
 BF16 = jnp.bfloat16
 VMEM_BYTES = 48 * 1024 * 1024
 ORDER = (
-    46, 20, 15, 26, 49, 35, 61, 0, 12, 56, 53, 18, 41, 7, 27, 34,
-    43, 54, 23, 8, 57, 28, 16, 36, 51, 62, 1, 31, 42, 13, 50, 44,
-    24, 9, 39, 21, 6, 59, 58, 14, 55, 22, 40, 60, 47, 3, 29, 32,
-    17, 52, 2, 25, 11, 37, 4, 45, 48, 10, 63, 33, 19, 30, 38, 5,
+    46, 20, 15, 26, 48, 29, 61, 0, 12, 56, 8, 18, 31, 7, 4, 17,
+    43, 54, 23, 53, 57, 28, 16, 36, 51, 62, 1, 41, 63, 13, 50, 10,
+    24, 9, 39, 27, 21, 6, 38, 58, 14, 52, 34, 32, 35, 3, 60, 47,
+    22, 40, 2, 55, 25, 19, 37, 45, 49, 44, 42, 5, 11, 30, 59, 33,
 )
 LAST_ORDER = (4, 1, 6, 2, 3, 7, 5, 0)
 
@@ -61,15 +61,17 @@
     return high, (value - high.astype(F32)).astype(BF16)
 
 
-def pack(order, x_ref, out_ref, sems):
+def pack(order, x_ref, out_ref, held_ref, sems):
     copies = [
-        pltpu.make_async_copy(x_ref.at[:, channel], out_ref.at[slot], sems.at[slot])
-        for slot, channel in enumerate(order)
+        pltpu.make_async_copy(x_ref.at[t], held_ref.at[t], sems.at[t])
+        for t in range(x_ref.shape[0])
     ]
     for copy in copies:
         copy.start()
-    for copy in copies:
+    for t, copy in enumerate(copies):
         copy.wait()
+        for slot, channel in enumerate(order):
+            out_ref[slot, t] = held_ref[t, channel]
 
 
 def rows_of(got_ref, slots, t):
@@ -141,7 +143,7 @@
         out_shape=pltpu.VMEM((channels, samples) + view.shape[2:], BF16),
         in_specs=[pl.BlockSpec(memory_space=pltpu.HBM)],
         out_specs=vmem,
-        scratch_shapes=[pltpu.SemaphoreType.DMA((channels,))],
+        scratch_shapes=[pltpu.VMEM(view.shape, BF16), pltpu.SemaphoreType.DMA((samples,))],
         compiler_params=params,
         name="pack",
     )(pltpu.with_memory_space_constraint(view, pltpu.HBM))

time: 77.4 us -> 76.7 us (level)
    all_to_all x1, blocking collectives: 59.8 us -> 57.4 us  [shards(): lax.all_to_all(sent, ('tm', 'ap'), 0, 0, axis_index_groups=groups, tiled=...]
    all_to_all x1, blocking collectives: 9.76 us -> 11.8 us  [shards(): lax.all_to_all(terms, 'tm', 0, 0, axis_index_groups=[list(last)], tiled=T...]
where the time goes in v8:
time: 76.7 us; the launch traced here: 76.3 us
  blocking collectives  69.2 us (90%)
  Pallas kernels  6.13 us (8%)
  local copies, waits for them, and re-layouts  0.8 us (1%)
    all_to_all x1, blocking collectives, shards(): lax.all_to_all(sent, ('tm', 'ap'), 0, 0, axis_index_groups=groups, tiled=...  57.4 us
    all_to_all x1, blocking collectives, shards(): lax.all_to_all(terms, 'tm', 0, 0, axis_index_groups=[list(last)], tiled=T...  11.8 us
    pallas_call x1, Pallas kernels, shards(): pl.pallas_call(functools.partial(correlate, slots, [last.index(t) for t i...  4.36 us
    pallas_call x1, Pallas kernels, shards(): pl.pallas_call(functools.partial(pack, order), out_shape=pltpu.VMEM((chan...  1.77 us

profile of v8, /device:TPU:16, one launch (start us, length us, event | category | flops | bytes accessed | tf_op | source)
XLA Modules:
  0.0 76.3 jit_solution(13391028753201990135)
XLA Ops:
  0.0 1.8 %pack.1 = bf16[64,16,8,128]{3,2,1,0:T(8,128)(2,1)S(1)} custom-call(bf16[16,64,8,128]{3,2,1,0:T(8,128)(2,1)} %bitcast.7), custom_call_target="tpu_custom_call" | custom-call | tf_op jit(solution)/shard_map/pack/pallas_call | solution.py:141
  1.8 0.0 copy-start
  1.8 0.0 copy-start.1
  1.8 0.0 copy-start.2
  1.8 0.0 copy-start.3
  1.8 0.0 copy-start.4
  1.8 0.0 copy-start.5
  1.9 57.4 %all_to_all.10.got_ref = bf16[64,16,8,128]{3,2,1,0:T(8,128)(2,1)S(1)} all-to-all(bf16[64,16,8,128]{3,2,1,0:T(8,128)(2,1)S(1)} %pack.1), channel_id=1, replica_groups={{184,80,57,104,192,113,241,0,48,224,32,72,121,25,16,65,169,216,89,209,2..., dimensions={0} | all-to-all | bytes 4194304 | tf_op jit(solution)/shard_map/all_to_all | solution.py:155
  59.3 0.0 copy-done
  59.3 0.0 copy-done.1
  59.3 0.0 copy-done.2
  59.3 0.0 copy-done.3
  59.3 0.0 copy-done.4
  59.3 0.0 copy-done.5
  59.3 4.4 %correlate.1 = bf16[8,2,32,256]{3,2,1,0:T(8,128)(2,1)S(1)} custom-call(bf16[64,16,8,128]{3,2,1,0:T(8,128)(2,1)S(1)} %all_to_all.10.got_ref, bf16[256,512]{1,0:T(8,128)(2,1)S(1)} %copy-done.3, bf16[512,256]{1,0:T(8,128)(2,1)S(1)} %copy-done.2, bf16[256,768]{1,0:T(8,128)(2,1)S(1)} %copy-done.1, bf16[768,512]{1,0:T(8,128)(2,1)S(1)} %copy-done, ...), custom_call_target="tpu_custom_call" | custom-call | tf_op jit(solution)/shard_map/correlate/pallas_call | solution.py:157
  63.7 11.8 %all_to_all.11 = bf16[8,2,32,256]{3,2,1,0:T(8,128)(2,1)S(1)} all-to-all(bf16[8,2,32,256]{3,2,1,0:T(8,128)(2,1)S(1)} %correlate.1), channel_id=1, replica_groups={{4,1,6,2,3,7,5,0},{12,9,14,10,11,15,13,8},{20,17,22,18,19,23,21,16},{28..., dimensions={0} | all-to-all | bytes 524288 | tf_op jit(solution)/shard_map/all_to_all | solution.py:166
  75.5 0.8 copy.9
  (2 shorter events, 0.0 us)
Async XLA Ops:
  1.8 57.5 %copy-start = (bf16[768,512]{1,0:T(8,128)(2,1)S(1)}, bf16[768,512]{1,0:T(8,128)(2,1)}, u32[]{:S(2)}) copy-start(bf16[768,512]{1,0:T(8,128)(2,1)} %constant.15.clone.by_col) | copy-start | bytes 2359300
  1.8 57.5 %copy-start.1 = (bf16[256,768]{1,0:T(8,128)(2,1)S(1)}, bf16[256,768]{1,0:T(8,128)(2,1)}, u32[]{:S(2)}) copy-start(bf16[256,768]{1,0:T(8,128)(2,1)} %constant.14.clone.by_row) | copy-start | bytes 1179652
  1.8 57.5 %copy-start.2 = (bf16[512,256]{1,0:T(8,128)(2,1)S(1)}, bf16[512,256]{1,0:T(8,128)(2,1)}, u32[]{:S(2)}) copy-start(bf16[512,256]{1,0:T(8,128)(2,1)} %constant.13.clone.second_ref) | copy-start | bytes 786436
  1.8 57.5 %copy-start.3 = (bf16[256,512]{1,0:T(8,128)(2,1)S(1)}, bf16[256,512]{1,0:T(8,128)(2,1)}, u32[]{:S(2)}) copy-start(bf16[256,512]{1,0:T(8,128)(2,1)} %constant.12.clone.first_ref) | copy-start | bytes 786436
  1.8 57.5 %copy-start.4 = (f32[128,256]{1,0:T(8,128)S(1)}, f32[128,256]{1,0:T(8,128)}, u32[]{:S(2)}) copy-start(f32[128,256]{1,0:T(8,128)} %constant.16.clone.factor_ref) | copy-start | bytes 393220
  1.8 57.5 %copy-start.5 = (bf16[128,128]{1,0:T(8,128)(2,1)S(1)}, bf16[128,128]{1,0:T(8,128)(2,1)}, u32[]{:S(2)}) copy-start(bf16[128,128]{1,0:T(8,128)(2,1)} %constant.17.clone.flip_ref) | copy-start | bytes 98308

commit v9 on v8

--- a/solution.py
+++ b/solution.py
@@ -125,6 +125,13 @@
             out_ref[places[near + i], part] = upper[i * owned : (i + 1) * owned, part * pad : (part + 1) * pad]
 
 
+def finish(senders, parts_ref, out_ref):
+    for p, places in enumerate(senders):
+        total = sum(parts_ref[i].astype(F32) for i in places)
+        for part in range(2):
+            out_ref[:, part, p] = total[part]
+
+
 def shards(voltages):
     samples, channels, local_rows, twice = voltages.shape
     grid_side = twice // 2
@@ -164,10 +171,15 @@
         name="correlate",
     )(got, *[jnp.asarray(c) for c in consts])
     parts = lax.all_to_all(terms, "tm", 0, 0, axis_index_groups=[list(last)], tiled=True)
-    sums = [
-        sum(parts[i].astype(F32) for i, t in enumerate(last) if t % own == p) for p in range(own)
-    ]
-    return jnp.stack(sums, 0).transpose(2, 1, 0, 3)
+    senders = [[i for i, t in enumerate(last) if t % own == p] for p in range(own)]
+    return pl.pallas_call(
+        functools.partial(finish, senders),
+        out_shape=jax.ShapeDtypeStruct((owned, 2, own, pad_side), F32),
+        in_specs=[vmem],
+        out_specs=vmem,
+        compiler_params=params,
+        name="finish",
+    )(parts)
 
 
 def solution(mesh):

time: 76.7 us -> 76.6 us (level)
  no operation moved by 1% of the time
where the time goes in v9:
time: 76.6 us; the launch traced here: 76.2 us
  blocking collectives  69.2 us (90%)
  Pallas kernels  6.85 us (9%)
    all_to_all x1, blocking collectives, shards(): lax.all_to_all(sent, ('tm', 'ap'), 0, 0, axis_index_groups=groups, tiled=...  57.4 us
    all_to_all x1, blocking collectives, shards(): lax.all_to_all(terms, 'tm', 0, 0, axis_index_groups=[list(last)], tiled=T...  11.8 us
    pallas_call x1, Pallas kernels, shards(): pl.pallas_call(functools.partial(correlate, slots, [last.index(t) for t i...  4.36 us
    pallas_call x1, Pallas kernels, shards(): pl.pallas_call(functools.partial(pack, order), out_shape=pltpu.VMEM((chan...  1.77 us

profile of v9, /device:TPU:16, one launch (start us, length us, event | category | flops | bytes accessed | tf_op | source)
XLA Modules:
  0.0 76.2 jit_solution(11699453487429763732)
XLA Ops:
  0.0 1.8 %pack.1 = bf16[64,16,8,128]{3,2,1,0:T(8,128)(2,1)S(1)} custom-call(bf16[16,64,8,128]{3,2,1,0:T(8,128)(2,1)} %bitcast.5), custom_call_target="tpu_custom_call" | custom-call | tf_op jit(solution)/shard_map/pack/pallas_call | solution.py:148
  1.8 0.0 copy-start
  1.8 0.0 copy-start.1
  1.8 0.0 copy-start.2
  1.8 0.0 copy-start.3
  1.8 0.0 copy-start.4
  1.8 0.0 copy-start.5
  1.9 57.4 %all_to_all.10.got_ref = bf16[64,16,8,128]{3,2,1,0:T(8,128)(2,1)S(1)} all-to-all(bf16[64,16,8,128]{3,2,1,0:T(8,128)(2,1)S(1)} %pack.1), channel_id=1, replica_groups={{184,80,57,104,192,113,241,0,48,224,32,72,121,25,16,65,169,216,89,209,2..., dimensions={0} | all-to-all | bytes 4194304 | tf_op jit(solution)/shard_map/all_to_all | solution.py:162
  59.3 0.0 copy-done
  59.3 0.0 copy-done.1
  59.3 0.0 copy-done.2
  59.3 0.0 copy-done.3
  59.3 0.0 copy-done.4
  59.3 0.0 copy-done.5
  59.3 4.4 %correlate.1 = bf16[8,2,32,256]{3,2,1,0:T(8,128)(2,1)S(1)} custom-call(bf16[64,16,8,128]{3,2,1,0:T(8,128)(2,1)S(1)} %all_to_all.10.got_ref, bf16[256,512]{1,0:T(8,128)(2,1)S(1)} %copy-done.3, bf16[512,256]{1,0:T(8,128)(2,1)S(1)} %copy-done.2, bf16[256,768]{1,0:T(8,128)(2,1)S(1)} %copy-done.1, bf16[768,512]{1,0:T(8,128)(2,1)S(1)} %copy-done, ...), custom_call_target="tpu_custom_call" | custom-call | tf_op jit(solution)/shard_map/correlate/pallas_call | solution.py:164
  63.7 11.8 %all_to_all.11.parts_ref = bf16[8,2,32,256]{3,2,1,0:T(8,128)(2,1)S(1)} all-to-all(bf16[8,2,32,256]{3,2,1,0:T(8,128)(2,1)S(1)} %correlate.1), channel_id=1, replica_groups={{4,1,6,2,3,7,5,0},{12,9,14,10,11,15,13,8},{20,17,22,18,19,23,21,16},{28..., dimensions={0} | all-to-all | bytes 524288 | tf_op jit(solution)/shard_map/all_to_all | solution.py:173
  75.5 0.7 finish.1
Async XLA Ops:
  1.8 57.5 %copy-start = (bf16[768,512]{1,0:T(8,128)(2,1)S(1)}, bf16[768,512]{1,0:T(8,128)(2,1)}, u32[]{:S(2)}) copy-start(bf16[768,512]{1,0:T(8,128)(2,1)} %constant.15.clone.by_col) | copy-start | bytes 2359300
  1.8 57.5 %copy-start.1 = (bf16[256,768]{1,0:T(8,128)(2,1)S(1)}, bf16[256,768]{1,0:T(8,128)(2,1)}, u32[]{:S(2)}) copy-start(bf16[256,768]{1,0:T(8,128)(2,1)} %constant.14.clone.by_row) | copy-start | bytes 1179652
  1.8 57.5 %copy-start.2 = (bf16[512,256]{1,0:T(8,128)(2,1)S(1)}, bf16[512,256]{1,0:T(8,128)(2,1)}, u32[]{:S(2)}) copy-start(bf16[512,256]{1,0:T(8,128)(2,1)} %constant.13.clone.second_ref) | copy-start | bytes 786436
  1.8 57.5 %copy-start.3 = (bf16[256,512]{1,0:T(8,128)(2,1)S(1)}, bf16[256,512]{1,0:T(8,128)(2,1)}, u32[]{:S(2)}) copy-start(bf16[256,512]{1,0:T(8,128)(2,1)} %constant.12.clone.first_ref) | copy-start | bytes 786436
  1.8 57.5 %copy-start.4 = (f32[128,256]{1,0:T(8,128)S(1)}, f32[128,256]{1,0:T(8,128)}, u32[]{:S(2)}) copy-start(f32[128,256]{1,0:T(8,128)} %constant.16.clone.factor_ref) | copy-start | bytes 393220
  1.8 57.5 %copy-start.5 = (bf16[128,128]{1,0:T(8,128)(2,1)S(1)}, bf16[128,128]{1,0:T(8,128)(2,1)}, u32[]{:S(2)}) copy-start(bf16[128,128]{1,0:T(8,128)(2,1)} %constant.17.clone.flip_ref) | copy-start | bytes 98308

commit v10 on v9

--- a/solution.py
+++ b/solution.py
@@ -62,16 +62,18 @@
 
 
 def pack(order, x_ref, out_ref, held_ref, sems):
-    copies = [
-        pltpu.make_async_copy(x_ref.at[t], held_ref.at[t], sems.at[t])
-        for t in range(x_ref.shape[0])
-    ]
+    chunk = x_ref.shape[0] // sems.shape[0]
+    copies = []
+    for i in range(sems.shape[0]):
+        at = pl.ds(i * chunk, chunk)
+        copies.append(pltpu.make_async_copy(x_ref.at[at], held_ref.at[at], sems.at[i]))
     for copy in copies:
         copy.start()
-    for t, copy in enumerate(copies):
+    for i, copy in enumerate(copies):
         copy.wait()
-        for slot, channel in enumerate(order):
-            out_ref[slot, t] = held_ref[t, channel]
+        for t in range(i * chunk, (i + 1) * chunk):
+            for slot, channel in enumerate(order):
+                out_ref[slot, t] = held_ref[t, channel]
 
 
 def rows_of(got_ref, slots, t):
@@ -150,7 +152,7 @@
         out_shape=pltpu.VMEM((channels, samples) + view.shape[2:], BF16),
         in_specs=[pl.BlockSpec(memory_space=pltpu.HBM)],
         out_specs=vmem,
-        scratch_shapes=[pltpu.VMEM(view.shape, BF16), pltpu.SemaphoreType.DMA((samples,))],
+        scratch_shapes=[pltpu.VMEM(view.shape, BF16), pltpu.SemaphoreType.DMA((math.gcd(samples, 8),))],
         compiler_params=params,
         name="pack",
     )(pltpu.with_memory_space_constraint(view, pltpu.HBM))

time: 76.6 us -> 76.5 us (level)
  no operation moved by 1% of the time
where the time goes in v10:
time: 76.5 us; the launch traced here: 76 us
  blocking collectives  69.2 us (90%)
  Pallas kernels  6.72 us (9%)
    all_to_all x1, blocking collectives, shards(): lax.all_to_all(sent, ('tm', 'ap'), 0, 0, axis_index_groups=groups, tiled=...  57.4 us
    all_to_all x1, blocking collectives, shards(): lax.all_to_all(terms, 'tm', 0, 0, axis_index_groups=[list(last)], tiled=T...  11.8 us
    pallas_call x1, Pallas kernels, shards(): pl.pallas_call(functools.partial(correlate, slots, [last.index(t) for t i...  4.36 us
    pallas_call x1, Pallas kernels, shards(): pl.pallas_call(functools.partial(pack, order), out_shape=pltpu.VMEM((chan...  1.64 us

profile of v10, /device:TPU:16, one launch (start us, length us, event | category | flops | bytes accessed | tf_op | source)
XLA Modules:
  0.0 76.0 jit_solution(13433296090378204572)
XLA Ops:
  0.0 1.6 %pack.1 = bf16[64,16,8,128]{3,2,1,0:T(8,128)(2,1)S(1)} custom-call(bf16[16,64,8,128]{3,2,1,0:T(8,128)(2,1)} %bitcast.5), custom_call_target="tpu_custom_call" | custom-call | tf_op jit(solution)/shard_map/pack/pallas_call | solution.py:150
  1.7 0.0 copy-start
  1.7 0.0 copy-start.1
  1.7 0.0 copy-start.2
  1.7 0.0 copy-start.3
  1.7 0.0 copy-start.4
  1.7 0.0 copy-start.5
  1.7 57.4 %all_to_all.10.got_ref = bf16[64,16,8,128]{3,2,1,0:T(8,128)(2,1)S(1)} all-to-all(bf16[64,16,8,128]{3,2,1,0:T(8,128)(2,1)S(1)} %pack.1), channel_id=1, replica_groups={{184,80,57,104,192,113,241,0,48,224,32,72,121,25,16,65,169,216,89,209,2..., dimensions={0} | all-to-all | bytes 4194304 | tf_op jit(solution)/shard_map/all_to_all | solution.py:164
  59.1 0.0 copy-done
  59.2 0.0 copy-done.1
  59.2 0.0 copy-done.2
  59.2 0.0 copy-done.3
  59.2 0.0 copy-done.4
  59.2 0.0 copy-done.5
  59.2 4.4 %correlate.1 = bf16[8,2,32,256]{3,2,1,0:T(8,128)(2,1)S(1)} custom-call(bf16[64,16,8,128]{3,2,1,0:T(8,128)(2,1)S(1)} %all_to_all.10.got_ref, bf16[256,512]{1,0:T(8,128)(2,1)S(1)} %copy-done.3, bf16[512,256]{1,0:T(8,128)(2,1)S(1)} %copy-done.2, bf16[256,768]{1,0:T(8,128)(2,1)S(1)} %copy-done.1, bf16[768,512]{1,0:T(8,128)(2,1)S(1)} %copy-done, ...), custom_call_target="tpu_custom_call" | custom-call | tf_op jit(solution)/shard_map/correlate/pallas_call | solution.py:166
  63.6 11.8 %all_to_all.11.parts_ref = bf16[8,2,32,256]{3,2,1,0:T(8,128)(2,1)S(1)} all-to-all(bf16[8,2,32,256]{3,2,1,0:T(8,128)(2,1)S(1)} %correlate.1), channel_id=1, replica_groups={{4,1,6,2,3,7,5,0},{12,9,14,10,11,15,13,8},{20,17,22,18,19,23,21,16},{28..., dimensions={0} | all-to-all | bytes 524288 | tf_op jit(solution)/shard_map/all_to_all | solution.py:175
  75.3 0.7 finish.1
Async XLA Ops:
  1.7 57.5 %copy-start = (bf16[768,512]{1,0:T(8,128)(2,1)S(1)}, bf16[768,512]{1,0:T(8,128)(2,1)}, u32[]{:S(2)}) copy-start(bf16[768,512]{1,0:T(8,128)(2,1)} %constant.15.clone.by_col) | copy-start | bytes 2359300
  1.7 57.5 %copy-start.1 = (bf16[256,768]{1,0:T(8,128)(2,1)S(1)}, bf16[256,768]{1,0:T(8,128)(2,1)}, u32[]{:S(2)}) copy-start(bf16[256,768]{1,0:T(8,128)(2,1)} %constant.14.clone.by_row) | copy-start | bytes 1179652
  1.7 57.5 %copy-start.2 = (bf16[512,256]{1,0:T(8,128)(2,1)S(1)}, bf16[512,256]{1,0:T(8,128)(2,1)}, u32[]{:S(2)}) copy-start(bf16[512,256]{1,0:T(8,128)(2,1)} %constant.13.clone.second_ref) | copy-start | bytes 786436
  1.7 57.5 %copy-start.3 = (bf16[256,512]{1,0:T(8,128)(2,1)S(1)}, bf16[256,512]{1,0:T(8,128)(2,1)}, u32[]{:S(2)}) copy-start(bf16[256,512]{1,0:T(8,128)(2,1)} %constant.12.clone.first_ref) | copy-start | bytes 786436
  1.7 57.5 %copy-start.4 = (f32[128,256]{1,0:T(8,128)S(1)}, f32[128,256]{1,0:T(8,128)}, u32[]{:S(2)}) copy-start(f32[128,256]{1,0:T(8,128)} %constant.16.clone.factor_ref) | copy-start | bytes 393220
  1.7 57.5 %copy-start.5 = (bf16[128,128]{1,0:T(8,128)(2,1)S(1)}, bf16[128,128]{1,0:T(8,128)(2,1)}, u32[]{:S(2)}) copy-start(bf16[128,128]{1,0:T(8,128)(2,1)} %constant.17.clone.flip_ref) | copy-start | bytes 98308

commit v11 on v10

--- a/solution.py
+++ b/solution.py
@@ -152,7 +152,7 @@
         out_shape=pltpu.VMEM((channels, samples) + view.shape[2:], BF16),
         in_specs=[pl.BlockSpec(memory_space=pltpu.HBM)],
         out_specs=vmem,
-        scratch_shapes=[pltpu.VMEM(view.shape, BF16), pltpu.SemaphoreType.DMA((math.gcd(samples, 8),))],
+        scratch_shapes=[pltpu.VMEM(view.shape, BF16), pltpu.SemaphoreType.DMA((math.gcd(samples, 4),))],
         compiler_params=params,
         name="pack",
     )(pltpu.with_memory_space_constraint(view, pltpu.HBM))

time: 76.5 us -> 76.6 us (level)
  no operation moved by 1% of the time
where the time goes in v11:
time: 76.6 us; the launch traced here: 76.1 us
  blocking collectives  69.2 us (90%)
  Pallas kernels  6.78 us (9%)
    all_to_all x1, blocking collectives, shards(): lax.all_to_all(sent, ('tm', 'ap'), 0, 0, axis_index_groups=groups, tiled=...  57.4 us
    all_to_all x1, blocking collectives, shards(): lax.all_to_all(terms, 'tm', 0, 0, axis_index_groups=[list(last)], tiled=T...  11.8 us
    pallas_call x1, Pallas kernels, shards(): pl.pallas_call(functools.partial(correlate, slots, [last.index(t) for t i...  4.37 us
    pallas_call x1, Pallas kernels, shards(): pl.pallas_call(functools.partial(pack, order), out_shape=pltpu.VMEM((chan...  1.7 us

profile of v11, /device:TPU:16, one launch (start us, length us, event | category | flops | bytes accessed | tf_op | source)
XLA Modules:
  0.0 76.1 jit_solution(1511875082920688422)
XLA Ops:
  0.0 1.7 %pack.1 = bf16[64,16,8,128]{3,2,1,0:T(8,128)(2,1)S(1)} custom-call(bf16[16,64,8,128]{3,2,1,0:T(8,128)(2,1)} %bitcast.5), custom_call_target="tpu_custom_call" | custom-call | tf_op jit(solution)/shard_map/pack/pallas_call | solution.py:150
  1.7 0.0 copy-start
  1.7 0.0 copy-start.1
  1.7 0.0 copy-start.2
  1.7 0.0 copy-start.3
  1.8 0.0 copy-start.4
  1.8 0.0 copy-start.5
  1.8 57.4 %all_to_all.10.got_ref = bf16[64,16,8,128]{3,2,1,0:T(8,128)(2,1)S(1)} all-to-all(bf16[64,16,8,128]{3,2,1,0:T(8,128)(2,1)S(1)} %pack.1), channel_id=1, replica_groups={{184,80,57,104,192,113,241,0,48,224,32,72,121,25,16,65,169,216,89,209,2..., dimensions={0} | all-to-all | bytes 4194304 | tf_op jit(solution)/shard_map/all_to_all | solution.py:164
  59.2 0.0 copy-done
  59.2 0.0 copy-done.1
  59.2 0.0 copy-done.2
  59.2 0.0 copy-done.3
  59.2 0.0 copy-done.4
  59.2 0.0 copy-done.5
  59.2 4.4 %correlate.1 = bf16[8,2,32,256]{3,2,1,0:T(8,128)(2,1)S(1)} custom-call(bf16[64,16,8,128]{3,2,1,0:T(8,128)(2,1)S(1)} %all_to_all.10.got_ref, bf16[256,512]{1,0:T(8,128)(2,1)S(1)} %copy-done.3, bf16[512,256]{1,0:T(8,128)(2,1)S(1)} %copy-done.2, bf16[256,768]{1,0:T(8,128)(2,1)S(1)} %copy-done.1, bf16[768,512]{1,0:T(8,128)(2,1)S(1)} %copy-done, ...), custom_call_target="tpu_custom_call" | custom-call | tf_op jit(solution)/shard_map/correlate/pallas_call | solution.py:166
  63.6 11.8 %all_to_all.11.parts_ref = bf16[8,2,32,256]{3,2,1,0:T(8,128)(2,1)S(1)} all-to-all(bf16[8,2,32,256]{3,2,1,0:T(8,128)(2,1)S(1)} %correlate.1), channel_id=1, replica_groups={{4,1,6,2,3,7,5,0},{12,9,14,10,11,15,13,8},{20,17,22,18,19,23,21,16},{28..., dimensions={0} | all-to-all | bytes 524288 | tf_op jit(solution)/shard_map/all_to_all | solution.py:175
  75.4 0.7 finish.1
Async XLA Ops:
  1.7 57.5 %copy-start = (bf16[768,512]{1,0:T(8,128)(2,1)S(1)}, bf16[768,512]{1,0:T(8,128)(2,1)}, u32[]{:S(2)}) copy-start(bf16[768,512]{1,0:T(8,128)(2,1)} %constant.15.clone.by_col) | copy-start | bytes 2359300
  1.7 57.5 %copy-start.1 = (bf16[256,768]{1,0:T(8,128)(2,1)S(1)}, bf16[256,768]{1,0:T(8,128)(2,1)}, u32[]{:S(2)}) copy-start(bf16[256,768]{1,0:T(8,128)(2,1)} %constant.14.clone.by_row) | copy-start | bytes 1179652
  1.7 57.5 %copy-start.2 = (bf16[512,256]{1,0:T(8,128)(2,1)S(1)}, bf16[512,256]{1,0:T(8,128)(2,1)}, u32[]{:S(2)}) copy-start(bf16[512,256]{1,0:T(8,128)(2,1)} %constant.13.clone.second_ref) | copy-start | bytes 786436
  1.7 57.5 %copy-start.3 = (bf16[256,512]{1,0:T(8,128)(2,1)S(1)}, bf16[256,512]{1,0:T(8,128)(2,1)}, u32[]{:S(2)}) copy-start(bf16[256,512]{1,0:T(8,128)(2,1)} %constant.12.clone.first_ref) | copy-start | bytes 786436
  1.8 57.5 %copy-start.4 = (f32[128,256]{1,0:T(8,128)S(1)}, f32[128,256]{1,0:T(8,128)}, u32[]{:S(2)}) copy-start(f32[128,256]{1,0:T(8,128)} %constant.16.clone.factor_ref) | copy-start | bytes 393220
  1.8 57.5 %copy-start.5 = (bf16[128,128]{1,0:T(8,128)(2,1)S(1)}, bf16[128,128]{1,0:T(8,128)(2,1)}, u32[]{:S(2)}) copy-start(bf16[128,128]{1,0:T(8,128)(2,1)} %constant.17.clone.flip_ref) | copy-start | bytes 98308

commit v12 on v11

--- a/solution.py
+++ b/solution.py
@@ -91,10 +91,10 @@
     samples = got_ref.shape[1]
     pad = second_ref.shape[1]
     grid_side = pad // 2
-    rows = [rows_of(got_ref, slots, t) for t in range(samples)]
+    rows = [rows_of(got_ref, senders, t) for senders in slots for t in range(samples)]
     field = dot(jnp.concatenate(rows, 0), first_ref[...]).astype(BF16)
     total = None
-    for t in range(samples):
+    for t in range(len(rows)):
         one = field[t * grid_side : (t + 1) * grid_side]
         beam = dot(second_ref[...], jnp.concatenate([one[:, :pad], one[:, pad:]], 0))
         power = beam[:pad] * beam[:pad] + beam[pad:] * beam[pad:]
@@ -107,9 +107,7 @@
     grid_side = pad // 2
     owned = out_ref.shape[2]
     near = grid_side // owned
-    for part, senders in enumerate(slots):
-        power = power_of(got_ref, first_ref, second_ref, senders)
-        power_ref[...] = power if part == 0 else power_ref[...] + power
+    power_ref[...] = power_of(got_ref, first_ref, second_ref, slots)
     high, low = halves(power_ref[...])
     half = dot(by_row[...], jnp.concatenate([high, low, high], 0))
     high, low = halves(half)

time: 76.6 us -> 76.6 us (level)
  no operation moved by 1% of the time
where the time goes in v12:
time: 76.6 us; the launch traced here: 76.1 us
  blocking collectives  69.2 us (90%)
  Pallas kernels  6.77 us (9%)
    all_to_all x1, blocking collectives, shards(): lax.all_to_all(sent, ('tm', 'ap'), 0, 0, axis_index_groups=groups, tiled=...  57.4 us
    all_to_all x1, blocking collectives, shards(): lax.all_to_all(terms, 'tm', 0, 0, axis_index_groups=[list(last)], tiled=T...  11.8 us
    pallas_call x1, Pallas kernels, shards(): pl.pallas_call(functools.partial(correlate, slots, [last.index(t) for t i...  4.35 us
    pallas_call x1, Pallas kernels, shards(): pl.pallas_call(functools.partial(pack, order), out_shape=pltpu.VMEM((chan...  1.7 us

profile of v12, /device:TPU:16, one launch (start us, length us, event | category | flops | bytes accessed | tf_op | source)
XLA Modules:
  0.0 76.1 jit_solution(13712887013801090764)
XLA Ops:
  0.0 1.7 %pack.1 = bf16[64,16,8,128]{3,2,1,0:T(8,128)(2,1)S(1)} custom-call(bf16[16,64,8,128]{3,2,1,0:T(8,128)(2,1)} %bitcast.5), custom_call_target="tpu_custom_call" | custom-call | tf_op jit(solution)/shard_map/pack/pallas_call | solution.py:148
  1.7 0.0 copy-start
  1.7 0.0 copy-start.1
  1.7 0.0 copy-start.2
  1.7 0.0 copy-start.3
  1.8 0.0 copy-start.4
  1.8 0.0 copy-start.5
  1.8 57.4 %all_to_all.10.got_ref = bf16[64,16,8,128]{3,2,1,0:T(8,128)(2,1)S(1)} all-to-all(bf16[64,16,8,128]{3,2,1,0:T(8,128)(2,1)S(1)} %pack.1), channel_id=1, replica_groups={{184,80,57,104,192,113,241,0,48,224,32,72,121,25,16,65,169,216,89,209,2..., dimensions={0} | all-to-all | bytes 4194304 | tf_op jit(solution)/shard_map/all_to_all | solution.py:162
  59.2 0.0 copy-done
  59.2 0.0 copy-done.1
  59.2 0.0 copy-done.2
  59.2 0.0 copy-done.3
  59.2 0.0 copy-done.4
  59.2 0.0 copy-done.5
  59.2 4.3 %correlate.1 = bf16[8,2,32,256]{3,2,1,0:T(8,128)(2,1)S(1)} custom-call(bf16[64,16,8,128]{3,2,1,0:T(8,128)(2,1)S(1)} %all_to_all.10.got_ref, bf16[256,512]{1,0:T(8,128)(2,1)S(1)} %copy-done.3, bf16[512,256]{1,0:T(8,128)(2,1)S(1)} %copy-done.2, bf16[256,768]{1,0:T(8,128)(2,1)S(1)} %copy-done.1, bf16[768,512]{1,0:T(8,128)(2,1)S(1)} %copy-done, ...), custom_call_target="tpu_custom_call" | custom-call | tf_op jit(solution)/shard_map/correlate/pallas_call | solution.py:164
  63.6 11.8 %all_to_all.11.parts_ref = bf16[8,2,32,256]{3,2,1,0:T(8,128)(2,1)S(1)} all-to-all(bf16[8,2,32,256]{3,2,1,0:T(8,128)(2,1)S(1)} %correlate.1), channel_id=1, replica_groups={{4,1,6,2,3,7,5,0},{12,9,14,10,11,15,13,8},{20,17,22,18,19,23,21,16},{28..., dimensions={0} | all-to-all | bytes 524288 | tf_op jit(solution)/shard_map/all_to_all | solution.py:173
  75.4 0.7 finish.1
Async XLA Ops:
  1.7 57.5 %copy-start = (bf16[768,512]{1,0:T(8,128)(2,1)S(1)}, bf16[768,512]{1,0:T(8,128)(2,1)}, u32[]{:S(2)}) copy-start(bf16[768,512]{1,0:T(8,128)(2,1)} %constant.15.clone.by_col) | copy-start | bytes 2359300
  1.7 57.5 %copy-start.1 = (bf16[256,768]{1,0:T(8,128)(2,1)S(1)}, bf16[256,768]{1,0:T(8,128)(2,1)}, u32[]{:S(2)}) copy-start(bf16[256,768]{1,0:T(8,128)(2,1)} %constant.14.clone.by_row) | copy-start | bytes 1179652
  1.7 57.5 %copy-start.2 = (bf16[512,256]{1,0:T(8,128)(2,1)S(1)}, bf16[512,256]{1,0:T(8,128)(2,1)}, u32[]{:S(2)}) copy-start(bf16[512,256]{1,0:T(8,128)(2,1)} %constant.13.clone.second_ref) | copy-start | bytes 786436
  1.7 57.5 %copy-start.3 = (bf16[256,512]{1,0:T(8,128)(2,1)S(1)}, bf16[256,512]{1,0:T(8,128)(2,1)}, u32[]{:S(2)}) copy-start(bf16[256,512]{1,0:T(8,128)(2,1)} %constant.12.clone.first_ref) | copy-start | bytes 786436
  1.8 57.5 %copy-start.4 = (f32[128,256]{1,0:T(8,128)S(1)}, f32[128,256]{1,0:T(8,128)}, u32[]{:S(2)}) copy-start(f32[128,256]{1,0:T(8,128)} %constant.16.clone.factor_ref) | copy-start | bytes 393220
  1.8 57.5 %copy-start.5 = (bf16[128,128]{1,0:T(8,128)(2,1)S(1)}, bf16[128,128]{1,0:T(8,128)(2,1)}, u32[]{:S(2)}) copy-start(bf16[128,128]{1,0:T(8,128)(2,1)} %constant.17.clone.flip_ref) | copy-start | bytes 98308
